TPU v7x, 512 devices: a whole 4x4x16 slice. The times are simulated.
512 devices in a mesh: gx: 16 (over z), gy: 8 (over x, core), gz: 4 (over y).
Axes of the slice: x: 4, y: 4, z: 16, core: 2. Of those that a mesh axis runs over, the one named last changes fastest.
Arguments:
- global_now: float32 [32, 6, 128, 128], P('gy', None, 'gx'), may hold values from -6 to 6
- global_prev: float32 [32, 6, 128, 128], P('gy', None, 'gx'), may hold values from -6 to 6
- cycle_modes: int32 [128], P('gx'), may hold values from 1 to 32
- wave_speed: float32 [128, 128], P('gx'), may hold values from 1 to 3
- inv_radius: float32 [128, 128], P('gx'), may hold values from 0.0005 to 0.005
- theta_second: float32 [128, 128], replicated, may hold values from -0.5 to 0.5
- theta_first: float32 [128, 128], replicated, may hold values from -0.5 to 0.5
- point_dest: int32 [4, 8192, 1], P('gz', 'gx'), may hold values from 0 to 127; in each aligned block of 512 rows (0 to 511, 512 to 1023, ..., all dimensions but the last counted through in order) at most 8 rows name the same one
- point_target: int32 [4, 8192], P('gz', 'gx'), may hold values from 0 to 4095
- point_source: int32 [4, 8192], P('gz', 'gx'), may hold values from 0 to 1023
- point_azimuth: float32 [4, 8192], P('gz', 'gx'), may hold values from -3.140625 to 3.140625
- regional_now: float32 [3, 64, 64, 512], P(None, 'gx', 'gy', 'gz'), may hold values from -6 to 6
- regional_prev: float32 [3, 64, 64, 512], P(None, 'gx', 'gy', 'gz'), may hold values from -6 to 6
- moduli: float32 [64, 64, 512], P('gx', 'gy', 'gz'), may hold values from 0.5 to 2
- inv_mass: float32 [64, 64, 512], P('gx', 'gy', 'gz'), may hold values from 0.5 to 2
Outputs:
- global_next: float32 [32, 6, 128, 128], P('gy', None, 'gx')
- regional_next: float32 [3, 64, 64, 512], P(None, 'gx', 'gy', 'gz')
- injected_force: float32 [3, 64, 64, 512], P(None, 'gx', 'gy', 'gz')
Inputs may be any that keep to these rules, and one draw needn't show every extreme that they name: `point_dest`: among the 512 points of one device (one aligned block of rows) at most 8 name one owner; in some block an owner is named exactly 8 times.
All inputs are finite; a program needn't handle non-finite values.
Results may differ from a plain program's by a relative error of at most 0.0003.
Values sent between devices are 32-bit elements; how exact they have to be, the bound alone decides.
A program may use at most 64 MiB of HBM per device.

v0:
```python
import functools
import math

import jax
import jax.numpy as jnp
import numpy as np
from jax import lax
from jax.experimental import pallas as pl
from jax.experimental.pallas import tpu as pltpu
from jax.sharding import PartitionSpec as P

F32 = jnp.float32
BF16 = jnp.bfloat16
MESH = pl.DeviceIdType.MESH

time_step = 0.3
time_sq = 0.09
impedance = 0.5
coupling = 0.05
slab_factor = 0.04

LANES = 128
RANKS = 8


def gll_products():
    nodes = np.array([-1.0, -math.sqrt(3.0 / 7.0), 0.0, math.sqrt(3.0 / 7.0), 1.0])
    weights = np.array([0.1, 49.0 / 90.0, 32.0 / 45.0, 49.0 / 90.0, 0.1])
    factor = np.array(
        [np.prod([nodes[i] - nodes[k] for k in range(5) if k != i]) for i in range(5)]
    )
    deriv = np.zeros((5, 5))
    for i in range(5):
        for j in range(5):
            if i != j:
                deriv[i, j] = factor[i] / factor[j] / (nodes[i] - nodes[j])
            else:
                deriv[i, j] = sum((1.0 / (nodes[i] - nodes[k]) for k in range(5) if k != i))
    return weights, np.einsum("ki,k,kj->kij", deriv, weights, deriv)


WEIGHTS, GRAM = gll_products()


def cosine_series():
    f = np.cos(np.linspace(0.0, np.pi / 2, 2001)) * 0.5
    fit = np.polynomial.chebyshev.Chebyshev.fit(f * f, np.cos(2 * np.pi * f), 8, domain=[0, 0.25])
    return [float(v) for v in fit.convert(kind=np.polynomial.Polynomial).coef]


COSINE = cosine_series()


def halves(x):
    high = x.astype(BF16)
    return high, (x - high.astype(F32)).astype(BF16)


def dot(a, b):
    return lax.dot_general(a, b, (((1,), (0,)), ((), ())), preferred_element_type=F32)


def dot_rows(a, b):
    return lax.dot_general(a, b, (((1,), (1,)), ((), ())), preferred_element_type=F32)


def operator_pair(t):
    high, low = halves(t)
    top = jnp.concatenate([high, low], axis=1)
    bottom = jnp.concatenate([high, jnp.zeros_like(low)], axis=1)
    return jnp.concatenate([top, bottom], axis=0)


def times_operator(x, pair_ref):
    high, low = halves(x)
    both = dot(jnp.concatenate([high, low], axis=1), pair_ref[...])
    return both[:, :LANES] + both[:, LANES:]


def iota(shape, axis):
    return lax.broadcasted_iota(jnp.int32, shape, axis)


def by_four(phase, values):
    out = jnp.full(phase.shape, values[3], F32)
    for i in (2, 1, 0):
        out = jnp.where(phase == i, F32(values[i]), out)
    return out


def kernel(
    sizes,
    modes_ref,
    now_in,
    prev_in,
    speed_in,
    radius_in,
    second_in,
    first_in,
    dest_in,
    target_in,
    source_in,
    azimuth_in,
    slab_in,
    before_in,
    moduli_in,
    mass_in,
    g_out,
    slab_out,
    force_out,
    now_ref,
    prev_ref,
    speed_ref,
    radius_ref,
    second_ref,
    first_ref,
    dest_ref,
    target_ref,
    source_ref,
    azimuth_ref,
    slab_ref,
    before_ref,
    moduli_ref,
    mass_ref,
    one_ref,
    two_ref,
    edge_ref,
    pair_second,
    pair_first,
    pick_ref,
    trig_ref,
    slot_ref,
    mark_ref,
    base_ref,
    force_ref,
    step_ref,
    last_ref,
    band_z,
    band_y,
    band_x,
    over_z,
    over_y,
    spread_ref,
    part_ref,
    cycle_send,
    cycle_recv,
    x_send,
    x_recv,
    y_send,
    y_recv,
    z_send,
    z_recv,
    group_send,
    group_recv,
    owner_send,
    owner_recv,
    in_sem,
    out_sem,
    cycle_sems,
    face_sems,
    group_sems,
    owner_sems,
):
    n_gx, n_gy, n_gz = sizes
    gx, gy, gz = lax.axis_index("gx"), lax.axis_index("gy"), lax.axis_index("gz")
    points = dest_ref.shape[1]

    loads = {}
    for number, (name, src, dst) in enumerate(
        (
            ("now", now_in, now_ref),
            ("prev", prev_in, prev_ref),
            ("speed", speed_in, speed_ref),
            ("radius", radius_in, radius_ref),
            ("moduli", moduli_in, moduli_ref),
            ("second", second_in, second_ref),
            ("dest", dest_in, dest_ref),
            ("target", target_in, target_ref),
            ("source", source_in, source_ref),
            ("azimuth", azimuth_in, azimuth_ref),
            ("first", first_in, first_ref),
            ("slab", slab_in, slab_ref),
            ("before", before_in, before_ref),
            ("mass", mass_in, mass_ref),
        )
    ):
        loads[name] = pltpu.make_async_copy(src, dst, in_sem.at[number])
        loads[name].start()

    def away(axis, step):
        index, count = {"gx": (gx, n_gx), "gy": (gy, n_gy), "gz": (gz, n_gz)}[axis]
        return {axis: lax.rem(index + step + count, count)}

    barrier = pltpu.get_barrier_semaphore()
    for axis, steps in (
        ("gx", range(1, n_gx)),
        ("gy", range(1, n_gy)),
        ("gz", sorted({1, n_gz - 1})),
    ):
        for step in steps:
            pl.semaphore_signal(
                barrier, inc=1, device_id=away(axis, step), device_id_type=MESH
            )
    greeted = n_gx - 1 + n_gy - 1 + len({1, n_gz - 1})

    def push(src, dst, sems, index, device):
        copy = pltpu.make_async_remote_copy(
            src_ref=src,
            dst_ref=dst,
            send_sem=sems.at[(0, *index)],
            recv_sem=sems.at[(1, *index)],
            device_id=device,
            device_id_type=MESH,
        )
        copy.start()
        return copy

    sub = iota((8, LANES), 0)
    lane = iota((8, LANES), 1)

    mode_base = (4 * gy).astype(F32)
    row24 = iota((24, LANES), 0)
    order24 = mode_base + (
        (row24 >= 6).astype(F32) + (row24 >= 12).astype(F32) + (row24 >= 18).astype(F32)
    )
    square24 = order24 * order24
    for name in ("now", "prev", "speed", "radius"):
        loads[name].wait()
    for side, (edge, inner) in enumerate(((0, 1), (7, 6))):
        count = modes_ref[edge].astype(F32)
        mask = jnp.where(order24 < count, F32(1.0), F32(0.0))
        speed = speed_ref[edge : edge + 1, :]
        radius = radius_ref[edge : edge + 1, :]
        at_edge = now_ref[pl.ds(edge, 24, stride=8), :]
        cycle_send[side, 0:24, :] = at_edge
        cycle_send[side, 24:48, :] = mask * (
            (2.0 - 2.0 * time_sq * speed - time_sq * square24 * radius) * at_edge
            - prev_ref[pl.ds(edge, 24, stride=8), :]
            + time_sq * speed * now_ref[pl.ds(inner, 24, stride=8), :]
        )
        cycle_send[side, 48:56, :] = jnp.where(
            sub == 0, jnp.broadcast_to(speed, (8, LANES)), jnp.full((8, LANES), count, F32)
        )

    pl.semaphore_wait(barrier, greeted)

    sent = []
    cycle_in = []
    for side, step in ((0, -1), (1, 1)):
        copy = push(
            cycle_send.at[side], cycle_recv.at[side], cycle_sems, (side,), away("gx", step)
        )
        sent.append(copy)
        cycle_in.append(copy)

    last_x = jnp.where(gx < n_gx - 1, F32(1.0), F32(0.0))
    last_y = jnp.where(gy < n_gy - 1, F32(1.0), F32(0.0))
    last_z = jnp.where(gz < n_gz - 1, F32(1.0), F32(0.0))
    has_x = jnp.where(gx > 0, F32(1.0), F32(0.0))
    has_y = jnp.where(gy > 0, F32(1.0), F32(0.0))
    has_z = jnp.where(gz > 0, F32(1.0), F32(0.0))

    def send_faces(number, x_count, y_count):
        copies = []
        for side, step in ((0, -1), (1, 1)):
            for place, (axis, src, dst) in enumerate(
                (
                    ("gx", x_send.at[number, side, 0:x_count], x_recv.at[number, side, 0:x_count]),
                    ("gy", y_send.at[number, side, 0:y_count], y_recv.at[number, side, 0:y_count]),
                    ("gz", z_send.at[number, side], z_recv.at[number, side]),
                )
            ):
                copies.append(
                    push(src, dst, face_sems, (number, 2 * place + side), away(axis, step))
                )
        sent.extend(copies)
        return copies

    def columns_to_lanes(columns):
        out = jnp.zeros((8, LANES), F32)
        for number, column in enumerate(columns):
            out = jnp.where(lane == number, jnp.broadcast_to(column, (8, LANES)), out)
        return out

    loads["moduli"].wait()
    inner = [float(GRAM[k, 4, 4]) for k in range(5)]
    mu = moduli_ref[...].reshape(4, 8, LANES)
    x_send[0, 0, 0] = mu[0]
    x_send[0, 1, 0] = last_x * (
        inner[0] * mu[0] + inner[1] * mu[1] + inner[2] * mu[2] + inner[3] * mu[3]
    )
    y_send[0, 0, 0:8] = jnp.zeros((8, LANES), F32)
    y_send[0, 1, 0:8] = jnp.zeros((8, LANES), F32)
    y_send[0, 0, 0:4] = moduli_ref[pl.ds(0, 4, stride=8), :]
    y_send[0, 1, 0:4] = last_y * sum(
        inner[k] * moduli_ref[pl.ds(4 + k, 4, stride=8), :] for k in range(4)
    )
    tail = by_four(lane & 3, inner[:4]) * jnp.where(lane >= LANES - 4, last_z, F32(0.0))
    z_send[0, 0] = columns_to_lanes([mu[x][:, 0:1] for x in range(4)])
    z_send[0, 1] = columns_to_lanes(
        [jnp.sum(tail * mu[x], axis=1, keepdims=True) for x in range(4)]
    )
    moduli_copies = send_faces(0, 1, 8)

    loads["second"].wait()
    pair_second[...] = operator_pair(second_ref[...])
    counts = jnp.zeros((8, LANES), F32)
    for row in range(8):
        counts = jnp.where(sub == row, modes_ref[row].astype(F32), counts)
    order = mode_base + iota((4, 8, LANES), 0).astype(F32)
    mask = jnp.where(order < counts[None], F32(1.0), F32(0.0))
    speed, radius = speed_ref[...][None], radius_ref[...][None]
    hold = (mask * (2.0 - 2.0 * time_sq * speed - time_sq * (order * order) * radius))[:, None]
    side_weight = (mask * (time_sq * speed))[:, None]
    bend_weight = (mask * time_sq)[:, None]
    mask = mask[:, None]

    def section_sum(now, prev):
        cells = now.reshape(24, 8, LANES)
        rows = iota((24, 8, LANES), 1)
        near = jnp.where(rows == 0, F32(0.0), pltpu.roll(cells, 1, 1)) + jnp.where(
            rows == 7, F32(0.0), pltpu.roll(cells, 7, 1)
        )
        return (
            hold * now.reshape(4, 6, 8, LANES)
            - mask * prev.reshape(4, 6, 8, LANES)
            + side_weight * near.reshape(4, 6, 8, LANES)
            + bend_weight * times_operator(now, pair_second).reshape(4, 6, 8, LANES)
        )

    one_ref[...] = section_sum(now_ref[...], prev_ref[...]).reshape(192, LANES)
    edge_ref[...] = jnp.zeros((192, LANES), F32)

    for name in ("dest", "target", "source", "azimuth"):
        loads[name].wait()
    owner = dest_ref[...]
    blocks = points // LANES
    named = (iota((LANES, points), 0) == owner).astype(F32)
    named_rows = jnp.concatenate(
        [named[:, b * LANES : (b + 1) * LANES] for b in range(blocks)], axis=0
    ).astype(BF16)
    before = (iota((LANES, LANES), 0) < iota((LANES, LANES), 1)).astype(F32)
    counted = dot(
        named_rows, jnp.concatenate([before, jnp.ones_like(before)], axis=1).astype(BF16)
    )
    ranks, offset = [], None
    for b in range(blocks):
        piece = counted[b * LANES : (b + 1) * LANES]
        place = piece[:, :LANES] if offset is None else piece[:, :LANES] + offset
        ranks.append(
            jnp.sum(named[:, b * LANES : (b + 1) * LANES] * place, axis=0, keepdims=True)
        )
        offset = piece[:, LANES:] if offset is None else offset + piece[:, LANES:]
    rank = jnp.concatenate(ranks, axis=1).astype(jnp.int32)
    if n_gy == 8:
        owner_x, owner_y = owner >> 3, owner & 7
    else:
        owner_x, owner_y = owner >> 1, owner & 1
    slot = owner_x * RANKS + rank
    slot_ref[...] = (iota((LANES, points), 0) == slot).astype(F32).astype(BF16)
    target = target_ref[...]
    mine = jnp.where(owner_y == gy, F32(1.0), F32(0.0))
    sub_p = iota((8, points), 0)
    marks = jnp.where(
        sub_p == 0,
        (target >> 7).astype(F32) * mine,
        jnp.where(sub_p == 1, (target & 127).astype(F32) * mine, F32(0.0)),
    )
    marked = dot_rows(marks.astype(BF16), slot_ref[...])
    mark_ref[...] = jnp.broadcast_to(128.0 * marked[0:1] + marked[1:2], (8, LANES))
    source = source_ref[...]
    picked = (iota((LANES, points), 0) == (source & 127)).astype(F32).astype(BF16)
    pick_ref[0:LANES, :] = picked
    pick_ref[LANES:, :] = picked
    turns = (mode_base + (sub_p & 3).astype(F32)) * (azimuth_ref[...] * (0.5 / math.pi))
    turns = turns - jnp.where(sub_p >= 4, F32(0.25), F32(0.0))
    turns = turns - jnp.floor(turns + 0.5)
    square = turns * turns
    wave = jnp.full(square.shape, COSINE[-1], F32)
    for value in COSINE[-2::-1]:
        wave = wave * square + value
    in_cycle = sub_p == (source >> 7)
    for row in range(8):
        trig_ref[row] = jnp.where(
            in_cycle, jnp.broadcast_to(wave[row : row + 1], (8, points)), F32(0.0)
        )
    loads["first"].wait()
    pair_first[...] = operator_pair(first_ref[...])

    for copy in cycle_in:
        copy.wait_recv()
    flags = (last_x, has_x)
    near_edges = [cycle_recv[side, 0:24, :] for side in range(2)]
    bends = times_operator(jnp.concatenate(near_edges, axis=0), pair_second)
    beyond = []
    for side, edge in ((0, 7), (1, 0)):
        tail_rows = cycle_recv[side, 48:56, :]
        speed24 = tail_rows[0:1]
        mask24 = jnp.where(order24 < tail_rows[1:2], F32(1.0), F32(0.0))
        edge_ref[pl.ds(edge, 24, stride=8), :] = flags[side] * near_edges[side]
        value = cycle_recv[side, 24:48, :] + mask24 * time_sq * (
            speed24 * now_ref[pl.ds(edge, 24, stride=8), :] + bends[24 * side : 24 * side + 24]
        )
        beyond.append(flags[side] * value)
    one = one_ref[...].reshape(4, 6, 8, LANES) + side_weight * edge_ref[...].reshape(
        4, 6, 8, LANES
    )
    one = one.reshape(192, LANES)
    for side, edge in ((0, 7), (1, 0)):
        edge_ref[pl.ds(edge, 24, stride=8), :] = beyond[side]
    two = section_sum(one, now_ref[...]) + side_weight * edge_ref[...].reshape(4, 6, 8, LANES)
    two = two.reshape(192, LANES)
    two_ref[...] = two
    outs = [pltpu.make_async_copy(two_ref, g_out, out_sem.at[0])]
    outs[0].start()

    coef = coupling * times_operator(two, pair_first) + (coupling * impedance / time_step) * (
        two - one
    )
    high, low = halves(coef)
    at_points = dot(jnp.concatenate([high, low], axis=1), pick_ref[...]).reshape(
        4, 6, 8, points
    )
    values = jnp.zeros((8, points), F32)
    for c in range(3):
        total = jnp.zeros((8, points), F32)
        for m in range(4):
            total = total + at_points[m, 2 * c] * trig_ref[m]
            total = total + at_points[m, 2 * c + 1] * trig_ref[4 + m]
        values = jnp.where(
            (sub_p & 3) == c,
            jnp.broadcast_to(jnp.sum(total, axis=0, keepdims=True), (8, points)),
            values,
        )
    by_group = jnp.concatenate(
        [
            jnp.where(owner_y == 2 * t + (sub_p >> 2), values, F32(0.0))
            for t in range(n_gy // 2)
        ],
        axis=0,
    )
    high, low = halves(by_group)
    packed = dot_rows(jnp.concatenate([high, low], axis=0), slot_ref[...])
    packed = packed[: 4 * n_gy] + packed[4 * n_gy :]
    for group in range(n_gy):
        group_send[group] = packed[4 * group : 4 * group + 4]
    for step in range(1, n_gy):
        peer = away("gy", step)
        sent.append(
            push(
                group_send.at[peer["gy"]],
                group_recv.at[step],
                group_sems,
                (step,),
                peer,
            )
        )
    group_in = sent[-(n_gy - 1) :]

    for copy in moduli_copies:
        copy.wait_recv()
    mu_next_x = last_x * x_recv[0, 0, 0]
    sum_prev_x = x_recv[0, 1, 0]
    lane4 = iota((4, 8, LANES), 2)
    sub4 = iota((4, 8, LANES), 1)
    side_w = [0.2] + [float(v) for v in WEIGHTS[1:4]]
    first_weight = -float(WEIGHTS[4])
    weight_y = by_four(sub & 3, side_w) + jnp.where(
        sub == 0, (1.0 - has_y) * first_weight, F32(0.0)
    )
    weight_z = by_four(lane & 3, side_w) + jnp.where(
        lane == 0, (1.0 - has_z) * first_weight, F32(0.0)
    )
    weight_x = [side_w[0] + (1.0 - has_x) * first_weight] + side_w[1:]

    def make_band(axis, position, count, following, preceding, weights, has, last, band, over):
        shifted = {0: mu}
        for t in range(-4, 5):
            if t:
                rolled = pltpu.roll(mu, (-t) % count, axis)
                if t > 0:
                    rolled = jnp.where(position == count - t, following, rolled)
                shifted[t] = rolled
        pos2 = position[0]
        phase = pos2 & 3
        later = pos2 > 3
        band_values = []
        for s in range(5):
            total = None
            for t in range(s - 4, 5):
                row = [
                    GRAM[i + t, i, i + s] if 0 <= i + t <= 4 and i + s <= 4 else 0.0
                    for i in range(4)
                ]
                pattern = by_four(phase, row)
                if s == 0 and t <= 0:
                    pattern = pattern + jnp.where(
                        (phase == 0) & later, F32(GRAM[4 + t, 4, 4]), F32(0.0)
                    )
                term = pattern[None] * shifted[t]
                total = term if total is None else total + term
            if s == 0:
                total = total + jnp.where(
                    position == 0, preceding + has * float(GRAM[4, 4, 4]) * mu, F32(0.0)
                )
            band_values.append(total * weights)
        crossing = jnp.zeros_like(mu)
        for s in range(1, 5):
            crossing = jnp.where(position == count - s, band_values[s], crossing)
            inside = jnp.where(position >= count - s, F32(0.0), band_values[s])
            behind = pltpu.roll(inside, s, axis)
            if 2 * s == count:
                band[s] = inside + behind
                band[4 + s] = jnp.zeros_like(inside)
            else:
                band[s] = inside
                band[4 + s] = behind
        over[...] = last * crossing
        band[0] = band_values[0]

    y_next = y_recv[0, 0, 0:8]
    y_prev = y_recv[0, 1, 0:8]
    z_next = z_recv[0, 0]
    z_prev = z_recv[0, 1]

    def rows_of(value):
        return jnp.concatenate(
            [jnp.broadcast_to(value[x : x + 1], (8, LANES))[None] for x in range(4)], axis=0
        )

    def columns_of(value):
        return jnp.concatenate(
            [jnp.broadcast_to(value[:, x : x + 1], (8, LANES))[None] for x in range(4)], axis=0
        )

    stacked = lambda scale: jnp.concatenate([(scale(x))[None] for x in range(4)], axis=0)
    make_band(
        2,
        lane4,
        LANES,
        last_z * columns_of(z_next),
        columns_of(z_prev),
        stacked(lambda x: weight_x[x] * weight_y),
        has_z,
        last_z,
        band_z,
        over_z,
    )
    make_band(
        1,
        sub4,
        8,
        last_y * rows_of(y_next),
        rows_of(y_prev),
        stacked(lambda x: weight_x[x] * weight_z),
        has_y,
        last_y,
        band_y,
        over_y,
    )
    weight_yz = weight_y * weight_z
    planes = [mu[x] for x in range(4)] + [mu_next_x]
    for i in range(4):
        for j in range(i, 5):
            value = sum(float(GRAM[k, i, j]) * planes[k] for k in range(5))
            if i == 0 and j == 0:
                value = value + sum_prev_x + has_x * float(GRAM[4, 4, 4]) * mu[0]
            if j == 4:
                value = last_x * value
            band_x[5 * i + j] = value * weight_yz
    for x in range(4):
        band_z[0, x] = band_z[0, x] + band_y[0, x] + band_x[6 * x]

    def coupling_x(i, j):
        return band_x[5 * min(i, j) + max(i, j)]

    def face_values(number, ref):
        field = ref[...].reshape(3, 4, 8, LANES)
        for c in range(3):
            x_send[number, 0, c] = field[c, 0]
            x_send[number, 1, c] = sum(coupling_x(i, 4) * field[c, i] for i in range(4))
        y_send[number, 0, 0:12] = ref[pl.ds(0, 12, stride=8), :]
        part_ref[...] = (over_y[...][None] * field).reshape(96, LANES)
        y_send[number, 1, 0:12] = sum(
            part_ref[pl.ds(4 + k, 12, stride=8), :] for k in range(4)
        )
        z_send[number, 0] = columns_to_lanes(
            [field[c, x][:, 0:1] for c in range(3) for x in range(4)]
        )
        z_send[number, 1] = columns_to_lanes(
            [
                jnp.sum(over_z[x] * field[c, x], axis=1, keepdims=True)
                for c in range(3)
                for x in range(4)
            ]
        )
        return send_faces(number, 3, 16)

    def inner_stiffness(ref):
        field = ref[...].reshape(3, 4, 8, LANES)
        out = []
        for x in range(4):
            plane = field[:, x]
            total = band_z[0, x] * plane
            for s in range(1, 5):
                total = total + band_z[s, x] * pltpu.roll(plane, LANES - s, 2)
                total = total + band_z[4 + s, x] * pltpu.roll(plane, s, 2)
                total = total + band_y[s, x] * pltpu.roll(plane, 8 - s, 1)
                if s < 4:
                    total = total + band_y[4 + s, x] * pltpu.roll(plane, s, 1)
            for j in range(4):
                if j != x:
                    total = total + coupling_x(x, j) * field[:, j]
            out.append(total)
        return out

    def outer_stiffness(number, copies, inside):
        for copy in copies:
            copy.wait_recv()
        y_first = y_recv[number, 1, 0:12]
        y_after = y_recv[number, 0, 0:12]
        spread_ref[pl.ds(0, 12, stride=8), :] = y_first
        for k in range(4):
            spread_ref[pl.ds(4 + k, 12, stride=8), :] = y_after
        spread = spread_ref[...].reshape(3, 4, 8, LANES)
        z_first, z_after = z_recv[number, 1], z_recv[number, 0]
        x_after, x_first = x_recv[number, 0], x_recv[number, 1]
        out = []
        for x in range(4):
            rows = []
            for c in range(3):
                at = 4 * c + x
                row = inside[x][c] + coupling_x(x, 4) * x_after[c]
                row = row + jnp.where(sub == 0, F32(1.0), over_y[x]) * spread[c, x]
                row = row + jnp.where(
                    lane == 0,
                    jnp.broadcast_to(z_first[:, at : at + 1], (8, LANES)),
                    over_z[x] * jnp.broadcast_to(z_after[:, at : at + 1], (8, LANES)),
                )
                if x == 0:
                    row = row + x_first[c]
                rows.append(row)
            out.append(rows)
        return out

    spread_ref[...] = jnp.zeros((96, LANES), F32)
    loads["slab"].wait()
    now_copies = face_values(1, slab_ref)

    for copy in group_in:
        copy.wait_recv()
    total = group_send[gy]
    for step in range(1, n_gy):
        total = total + group_recv[step]
    rows16 = iota((n_gx, LANES), 0)
    lanes16 = iota((n_gx, LANES), 1)
    outgoing = jnp.zeros((n_gx, LANES), F32)
    for c in range(4):
        line = total[c : c + 1] if c < 3 else mark_ref[0:1]
        line = jnp.broadcast_to(line, (8, LANES))
        if (RANKS * (c + 1 - n_gx)) % LANES:
            line = pltpu.roll(line, (RANKS * (c + 1 - n_gx)) % LANES, 1)
        moved = pltpu.roll(
            jnp.broadcast_to(line[0:1], (n_gx, LANES)), 0, 1, stride=RANKS, stride_axis=0
        )
        outgoing = jnp.where(lanes16 >> 3 == c, moved, outgoing)
    owner_send[...] = outgoing.reshape(n_gx, 1, LANES)
    for step in range(1, n_gx):
        peer = away("gx", step)
        sent.append(
            push(
                owner_send.at[n_gx - 1 - peer["gx"]],
                owner_recv.at[step],
                owner_sems,
                (step,),
                peer,
            )
        )
    owner_in = sent[-(n_gx - 1) :]
    owner_recv[0] = owner_send[n_gx - 1 - gx]

    inside = inner_stiffness(slab_ref)
    loads["before"].wait()
    loads["mass"].wait()
    around = outer_stiffness(1, now_copies, inside)
    for x in range(4):
        scale = slab_factor * mass_ref[8 * x : 8 * x + 8, :]
        for c in range(3):
            at = 32 * c + 8 * x
            base_ref[at : at + 8, :] = (
                2.0 * slab_ref[at : at + 8, :]
                - before_ref[at : at + 8, :]
                - scale * around[x][c]
            )

    for copy in owner_in:
        copy.wait_recv()
    arrived = owner_recv[...].reshape(n_gx, LANES)
    lines = []
    moved = pltpu.roll(arrived, 0, 1, stride=RANKS, stride_axis=0)
    for c in range(4):
        own = ((lanes16 >> 3) - rows16 - c) & 15 == 0
        line = jnp.sum(jnp.where(own, moved, F32(0.0)), axis=0, keepdims=True)
        if c:
            line = pltpu.roll(jnp.broadcast_to(line, (8, LANES)), LANES - RANKS * c, 1)[0:1]
        lines.append(line)
    goal = lines[3].astype(jnp.int32)
    goal_row, goal_lane = goal >> 7, goal & 127
    rows32 = iota((32, LANES), 0)
    spots = jnp.concatenate(
        [jnp.where(rows32 == goal_row, lines[c], F32(0.0)) for c in range(3)], axis=0
    )
    high, low = halves(spots)
    on_lane = (iota((LANES, LANES), 0) == goal_lane).astype(F32).astype(BF16)
    force = dot_rows(
        jnp.concatenate([high, low], axis=1), jnp.concatenate([on_lane, on_lane], axis=1)
    )
    force_ref[...] = force
    outs.append(pltpu.make_async_copy(force_ref, force_out, out_sem.at[1]))
    outs[1].start()
    for x in range(4):
        scale = slab_factor * mass_ref[8 * x : 8 * x + 8, :]
        for c in range(3):
            at = 32 * c + 8 * x
            step_ref[at : at + 8, :] = base_ref[at : at + 8, :] + scale * force[at : at + 8]

    step_copies = face_values(2, step_ref)
    inside = inner_stiffness(step_ref)
    around = outer_stiffness(2, step_copies, inside)
    for x in range(4):
        scale = slab_factor * mass_ref[8 * x : 8 * x + 8, :]
        for c in range(3):
            at = 32 * c + 8 * x
            last_ref[at : at + 8, :] = (
                2.0 * step_ref[at : at + 8, :]
                - slab_ref[at : at + 8, :]
                + scale * (force_ref[at : at + 8, :] - around[x][c])
            )
    outs.append(pltpu.make_async_copy(last_ref, slab_out, out_sem.at[2]))
    outs[2].start()
    for copy in sent:
        copy.wait_send()
    for copy in outs:
        copy.wait()


def solution(mesh):
    n_gx, n_gy, n_gz = (mesh.shape[name] for name in ("gx", "gy", "gz"))

    def on_device(
        global_now,
        global_prev,
        cycle_modes,
        wave_speed,
        inv_radius,
        theta_second,
        theta_first,
        point_dest,
        point_target,
        point_source,
        point_azimuth,
        regional_now,
        regional_prev,
        moduli,
        inv_mass,
    ):
        points = point_target.shape[1]
        big = [((192, LANES), F32)] * 2 + [((8, LANES), F32)] * 2 + [((LANES, LANES), F32)] * 2
        big += [((1, points), jnp.int32)] * 3 + [((1, points), F32)]
        big += [((96, LANES), F32)] * 2 + [((32, LANES), F32)] * 2
        scratch = [pltpu.VMEM(shape, dtype) for shape, dtype in big]
        scratch += [
            pltpu.VMEM((192, LANES), F32),
            pltpu.VMEM((192, LANES), F32),
            pltpu.VMEM((192, LANES), F32),
            pltpu.VMEM((2 * LANES, 2 * LANES), BF16),
            pltpu.VMEM((2 * LANES, 2 * LANES), BF16),
            pltpu.VMEM((2 * LANES, points), BF16),
            pltpu.VMEM((8, 8, points), F32),
            pltpu.VMEM((LANES, points), BF16),
            pltpu.VMEM((8, LANES), F32),
            pltpu.VMEM((96, LANES), F32),
            pltpu.VMEM((96, LANES), F32),
            pltpu.VMEM((96, LANES), F32),
            pltpu.VMEM((96, LANES), F32),
            pltpu.VMEM((9, 4, 8, LANES), F32),
            pltpu.VMEM((9, 4, 8, LANES), F32),
            pltpu.VMEM((20, 8, LANES), F32),
            pltpu.VMEM((4, 8, LANES), F32),
            pltpu.VMEM((4, 8, LANES), F32),
            pltpu.VMEM((96, LANES), F32),
            pltpu.VMEM((96, LANES), F32),
            pltpu.VMEM((2, 56, LANES), F32),
            pltpu.VMEM((2, 56, LANES), F32),
            pltpu.VMEM((3, 2, 3, 8, LANES), F32),
            pltpu.VMEM((3, 2, 3, 8, LANES), F32),
            pltpu.VMEM((3, 2, 16, LANES), F32),
            pltpu.VMEM((3, 2, 16, LANES), F32),
            pltpu.VMEM((3, 2, 8, LANES), F32),
            pltpu.VMEM((3, 2, 8, LANES), F32),
            pltpu.VMEM((n_gy, 4, LANES), F32),
            pltpu.VMEM((n_gy, 4, LANES), F32),
            pltpu.VMEM((n_gx, 1, LANES), F32),
            pltpu.VMEM((n_gx, 1, LANES), F32),
            pltpu.SemaphoreType.DMA((14,)),
            pltpu.SemaphoreType.DMA((3,)),
            pltpu.SemaphoreType.DMA((2, 2)),
            pltpu.SemaphoreType.DMA((2, 3, 6)),
            pltpu.SemaphoreType.DMA((2, n_gy)),
            pltpu.SemaphoreType.DMA((2, n_gx)),
        ]
        hbm = pl.BlockSpec(memory_space=pl.ANY)
        two, slab, force = pl.pallas_call(
            functools.partial(kernel, (n_gx, n_gy, n_gz)),
            out_shape=[
                jax.ShapeDtypeStruct((192, LANES), F32),
                jax.ShapeDtypeStruct((96, LANES), F32),
                jax.ShapeDtypeStruct((96, LANES), F32),
            ],
            in_specs=[pl.BlockSpec(memory_space=pltpu.SMEM)] + [hbm] * 14,
            out_specs=[hbm] * 3,
            scratch_shapes=scratch,
            compiler_params=pltpu.CompilerParams(
                collective_id=0, has_side_effects=True, vmem_limit_bytes=48 * 2**20
            ),
        )(
            cycle_modes,
            global_now.reshape(192, LANES),
            global_prev.reshape(192, LANES),
            wave_speed,
            inv_radius,
            theta_second,
            theta_first,
            point_dest.reshape(1, points),
            point_target,
            point_source,
            point_azimuth,
            regional_now.reshape(96, LANES),
            regional_prev.reshape(96, LANES),
            moduli.reshape(32, LANES),
            inv_mass.reshape(32, LANES),
        )
        return (
            two.reshape(global_now.shape),
            slab.reshape(regional_now.shape),
            force.reshape(regional_now.shape),
        )

    return jax.shard_map(
        on_device,
        mesh=mesh,
        in_specs=(
            P("gy", None, "gx", None),
            P("gy", None, "gx", None),
            P("gx"),
            P("gx", None),
            P("gx", None),
            P(),
            P(),
            P("gz", "gx", None),
            P("gz", "gx"),
            P("gz", "gx"),
            P("gz", "gx"),
            P(None, "gx", "gy", "gz"),
            P(None, "gx", "gy", "gz"),
            P("gx", "gy", "gz"),
            P("gx", "gy", "gz"),
        ),
        out_specs=(P("gy", None, "gx", None), P(None, "gx", "gy", "gz"), P(None, "gx", "gy", "gz")),
        check_vma=False,
    )
```

profile of v0, /device:TPU:1, one launch (start us, length us, event | category | flops | bytes accessed | tf_op | source)
XLA Modules:
  0.0 48.1 jit_solution(15684949455446588370)
XLA Ops:
  0.6 0.0 copy-start.11
  0.6 0.0 copy-start.10
  0.7 0.0 copy-start.9
  0.7 0.0 copy-start.8
  0.7 0.0 copy-start.14
  0.7 0.6 %copy-done.11 = s32[1,512]{1,0:T(1,128)S(1)} copy-done((s32[1,512]{1,0:T(1,128)S(1)}, s32[1,512]{1,0:T(1,128)}, u32[]{:S(2)}) %copy-start.11) | copy-done | bytes 2072
  1.3 0.0 copy-done.10
  1.3 0.0 copy-done.9
  1.4 0.0 copy-done.8
  1.4 0.0 copy-done.14
  1.4 0.9 %copy-done = f32[4,6,8,128]{3,2,1,0:T(8,128)S(1)} copy-done((f32[4,6,8,128]{3,2,1,0:T(8,128)S(1)}, f32[4,6,8,128]{3,2,1,0:T(8,128)}, u32[]{:S(2)}) %copy-start) | copy-done | bytes 98328
  2.3 0.9 %copy-done.1 = f32[4,6,8,128]{3,2,1,0:T(8,128)S(1)} copy-done((f32[4,6,8,128]{3,2,1,0:T(8,128)S(1)}, f32[4,6,8,128]{3,2,1,0:T(8,128)}, u32[]{:S(2)}) %copy-start.1) | copy-done | bytes 98328
  3.2 0.8 %copy-done.2 = f32[128,128]{1,0:T(8,128)S(1)} copy-done((f32[128,128]{1,0:T(8,128)S(1)}, f32[128,128]{1,0:T(8,128)}, u32[]{:S(2)}) %copy-start.2) | copy-done | bytes 65560
  4.0 0.8 %copy-done.3 = f32[128,128]{1,0:T(8,128)S(1)} copy-done((f32[128,128]{1,0:T(8,128)S(1)}, f32[128,128]{1,0:T(8,128)}, u32[]{:S(2)}) %copy-start.3) | copy-done | bytes 65560
  4.8 0.8 %copy-done.4 = f32[3,4,8,128]{3,2,1,0:T(8,128)S(1)} copy-done((f32[3,4,8,128]{3,2,1,0:T(8,128)S(1)}, f32[3,4,8,128]{3,2,1,0:T(8,128)}, u32[]{:S(2)}) %copy-start.4) | copy-done | bytes 49176
  5.6 0.8 %copy-done.5 = f32[3,4,8,128]{3,2,1,0:T(8,128)S(1)} copy-done((f32[3,4,8,128]{3,2,1,0:T(8,128)S(1)}, f32[3,4,8,128]{3,2,1,0:T(8,128)}, u32[]{:S(2)}) %copy-start.5) | copy-done | bytes 49176
  6.4 0.7 %copy-done.6 = f32[4,8,128]{2,1,0:T(8,128)S(1)} copy-done((f32[4,8,128]{2,1,0:T(8,128)S(1)}, f32[4,8,128]{2,1,0:T(8,128)}, u32[]{:S(2)}) %copy-start.6) | copy-done | bytes 16408
  7.2 0.7 %copy-done.7 = f32[4,8,128]{2,1,0:T(8,128)S(1)} copy-done((f32[4,8,128]{2,1,0:T(8,128)S(1)}, f32[4,8,128]{2,1,0:T(8,128)}, u32[]{:S(2)}) %copy-start.7) | copy-done | bytes 16408
  7.9 0.7 %copy-done.12 = s32[1,512]{1,0:T(1,128)S(1)} copy-done((s32[1,512]{1,0:T(1,128)S(1)}, s32[1,512]{1,0:T(1,128)}, u32[]{:S(2)}) %copy-start.12) | copy-done | bytes 2072
  8.6 0.7 %copy-done.13 = f32[1,512]{1,0:T(1,128)S(1)} copy-done((f32[1,512]{1,0:T(1,128)S(1)}, f32[1,512]{1,0:T(1,128)}, u32[]{:S(2)}) %copy-start.13) | copy-done | bytes 2072
  9.2 36.9 %shard_map.166 = (f32[192,128]{1,0:T(8,128)S(1)}, f32[96,128]{1,0:T(8,128)S(1)}, f32[96,128]{1,0:T(8,128)S(1)}) custom-call(s32[8]{0:T(128)S(1)} %copy-done.14, f32[192,128]{1,0:T(8,128)S(1)} %bitcast.11, f32[192,128]{1,0:T(8,128)S(1)} %bitcast.12, f32[8,128]{1,0:T(8,128)S(1)} %copy-done.8, f32[8,128]{1,0:T(8,128)S(1)} %copy-done.9, ...), custom_call_target="tpu_custom_call" | custom-call | tf_op jit(solution)/shard_map/pallas_call | solution.py:813
  46.2 0.6 %copy.21 = f32[4,6,8,128]{3,2,1,0:T(8,128)} copy(f32[4,6,8,128]{3,2,1,0:T(8,128)S(1)} %bitcast.10) | data formatting | bytes 196608
  46.8 0.6 %copy.22 = f32[3,4,8,128]{3,2,1,0:T(8,128)} copy(f32[3,4,8,128]{3,2,1,0:T(8,128)S(1)} %bitcast.16) | data formatting | bytes 98304
  47.5 0.6 %copy.23 = f32[3,4,8,128]{3,2,1,0:T(8,128)} copy(f32[3,4,8,128]{3,2,1,0:T(8,128)S(1)} %bitcast.15) | data formatting | bytes 98304
  (10 shorter events, 0.0 us)
Async XLA Ops:
  0.6 0.7 %copy-start.11 = (s32[1,512]{1,0:T(1,128)S(1)}, s32[1,512]{1,0:T(1,128)}, u32[]{:S(2)}) copy-start(s32[1,512]{1,0:T(1,128)} %target_in.1) | copy-start | bytes 6148
  0.6 0.7 %copy-start.10 = (s32[1,512,1]{1,2,0:T(1,128)S(1)}, s32[1,512,1]{1,2,0:T(1,128)}, u32[]{:S(2)}) copy-start(s32[1,512,1]{1,2,0:T(1,128)} %param.22) | copy-start | bytes 6148
  0.7 0.7 %copy-start.9 = (f32[8,128]{1,0:T(8,128)S(1)}, f32[8,128]{1,0:T(8,128)}, u32[]{:S(2)}) copy-start(f32[8,128]{1,0:T(8,128)} %radius_in.1) | copy-start | bytes 12292
  0.7 0.7 %copy-start.8 = (f32[8,128]{1,0:T(8,128)S(1)}, f32[8,128]{1,0:T(8,128)}, u32[]{:S(2)}) copy-start(f32[8,128]{1,0:T(8,128)} %speed_in.1) | copy-start | bytes 12292
  0.7 0.7 %copy-start.14 = (s32[8]{0:T(128)S(1)}, s32[8]{0:T(128)}, u32[]{:S(2)}) copy-start(s32[8]{0:T(128)} %modes_ref.1) | copy-start | bytes 100
  1.4 0.9 %copy-start = (f32[4,6,8,128]{3,2,1,0:T(8,128)S(1)}, f32[4,6,8,128]{3,2,1,0:T(8,128)}, u32[]{:S(2)}) copy-start(f32[4,6,8,128]{3,2,1,0:T(8,128)} %param.15) | copy-start | bytes 294916
  2.3 0.9 %copy-start.1 = (f32[4,6,8,128]{3,2,1,0:T(8,128)S(1)}, f32[4,6,8,128]{3,2,1,0:T(8,128)}, u32[]{:S(2)}) copy-start(f32[4,6,8,128]{3,2,1,0:T(8,128)} %param.16) | copy-start | bytes 294916
  3.2 0.8 %copy-start.2 = (f32[128,128]{1,0:T(8,128)S(1)}, f32[128,128]{1,0:T(8,128)}, u32[]{:S(2)}) copy-start(f32[128,128]{1,0:T(8,128)} %second_in.1) | copy-start | bytes 196612
  4.0 0.8 %copy-start.3 = (f32[128,128]{1,0:T(8,128)S(1)}, f32[128,128]{1,0:T(8,128)}, u32[]{:S(2)}) copy-start(f32[128,128]{1,0:T(8,128)} %first_in.1) | copy-start | bytes 196612
  4.8 0.8 %copy-start.4 = (f32[3,4,8,128]{3,2,1,0:T(8,128)S(1)}, f32[3,4,8,128]{3,2,1,0:T(8,128)}, u32[]{:S(2)}) copy-start(f32[3,4,8,128]{3,2,1,0:T(8,128)} %param.26) | copy-start | bytes 147460
  5.6 0.8 %copy-start.5 = (f32[3,4,8,128]{3,2,1,0:T(8,128)S(1)}, f32[3,4,8,128]{3,2,1,0:T(8,128)}, u32[]{:S(2)}) copy-start(f32[3,4,8,128]{3,2,1,0:T(8,128)} %param.27) | copy-start | bytes 147460
  6.4 0.7 %copy-start.6 = (f32[4,8,128]{2,1,0:T(8,128)S(1)}, f32[4,8,128]{2,1,0:T(8,128)}, u32[]{:S(2)}) copy-start(f32[4,8,128]{2,1,0:T(8,128)} %param.28) | copy-start | bytes 49156
  7.2 0.7 %copy-start.7 = (f32[4,8,128]{2,1,0:T(8,128)S(1)}, f32[4,8,128]{2,1,0:T(8,128)}, u32[]{:S(2)}) copy-start(f32[4,8,128]{2,1,0:T(8,128)} %param.29) | copy-start | bytes 49156
  7.9 0.7 %copy-start.12 = (s32[1,512]{1,0:T(1,128)S(1)}, s32[1,512]{1,0:T(1,128)}, u32[]{:S(2)}) copy-start(s32[1,512]{1,0:T(1,128)} %source_in.1) | copy-start | bytes 6148
  8.6 0.7 %copy-start.13 = (f32[1,512]{1,0:T(1,128)S(1)}, f32[1,512]{1,0:T(1,128)}, u32[]{:S(2)}) copy-start(f32[1,512]{1,0:T(1,128)} %azimuth_in.1) | copy-start | bytes 6148
where the time goes:
time: 48.6 us; the launch traced here: 48.1 us
  Pallas kernels  36.9 us (76%)
  local copies, waits for them, and re-layouts  10.4 us (21%)
  between operations  0.7 us (1%)
    pallas_call x1, Pallas kernels, on_device(): pl.pallas_call(functools.partial(kernel, (n_gx, n_gy, n_gz)), out_shape=[...  36.9 us
    unnamed x33, local copies, waits for them, and re-layouts  10.4 us

commit v1 on v0

--- a/solution.py
+++ b/solution.py
@@ -90,7 +90,7 @@
 
 def kernel(
     sizes,
-    modes_ref,
+    modes_in,
     now_in,
     prev_in,
     speed_in,
@@ -108,6 +108,7 @@
     g_out,
     slab_out,
     force_out,
+    modes_ref,
     now_ref,
     prev_ref,
     speed_ref,
@@ -168,6 +169,7 @@
     loads = {}
     for number, (name, src, dst) in enumerate(
         (
+            ("modes", modes_in, modes_ref),
             ("now", now_in, now_ref),
             ("prev", prev_in, prev_ref),
             ("speed", speed_in, speed_ref),
@@ -224,7 +226,7 @@
         (row24 >= 6).astype(F32) + (row24 >= 12).astype(F32) + (row24 >= 18).astype(F32)
     )
     square24 = order24 * order24
-    for name in ("now", "prev", "speed", "radius"):
+    for name in ("modes", "now", "prev", "speed", "radius"):
         loads[name].wait()
     for side, (edge, inner) in enumerate(((0, 1), (7, 6))):
         count = modes_ref[edge].astype(F32)
@@ -744,6 +746,15 @@
         copy.wait()
 
 
+def copy_out(*refs):
+    sems = refs[6]
+    copies = [pltpu.make_async_copy(refs[i], refs[3 + i], sems.at[i]) for i in range(3)]
+    for copy in copies:
+        copy.start()
+    for copy in copies:
+        copy.wait()
+
+
 def solution(mesh):
     n_gx, n_gy, n_gz = (mesh.shape[name] for name in ("gx", "gy", "gz"))
 
@@ -768,7 +779,8 @@
         big = [((192, LANES), F32)] * 2 + [((8, LANES), F32)] * 2 + [((LANES, LANES), F32)] * 2
         big += [((1, points), jnp.int32)] * 3 + [((1, points), F32)]
         big += [((96, LANES), F32)] * 2 + [((32, LANES), F32)] * 2
-        scratch = [pltpu.VMEM(shape, dtype) for shape, dtype in big]
+        scratch = [pltpu.SMEM(cycle_modes.shape, jnp.int32)]
+        scratch += [pltpu.VMEM(shape, dtype) for shape, dtype in big]
         scratch += [
             pltpu.VMEM((192, LANES), F32),
             pltpu.VMEM((192, LANES), F32),
@@ -802,7 +814,7 @@
             pltpu.VMEM((n_gy, 4, LANES), F32),
             pltpu.VMEM((n_gx, 1, LANES), F32),
             pltpu.VMEM((n_gx, 1, LANES), F32),
-            pltpu.SemaphoreType.DMA((14,)),
+            pltpu.SemaphoreType.DMA((15,)),
             pltpu.SemaphoreType.DMA((3,)),
             pltpu.SemaphoreType.DMA((2, 2)),
             pltpu.SemaphoreType.DMA((2, 3, 6)),
@@ -813,17 +825,20 @@
         two, slab, force = pl.pallas_call(
             functools.partial(kernel, (n_gx, n_gy, n_gz)),
             out_shape=[
-                jax.ShapeDtypeStruct((192, LANES), F32),
-                jax.ShapeDtypeStruct((96, LANES), F32),
-                jax.ShapeDtypeStruct((96, LANES), F32),
+                pltpu.VMEM((192, LANES), F32),
+                pltpu.VMEM((96, LANES), F32),
+                pltpu.VMEM((96, LANES), F32),
             ],
-            in_specs=[pl.BlockSpec(memory_space=pltpu.SMEM)] + [hbm] * 14,
+            in_specs=[hbm] * 15,
             out_specs=[hbm] * 3,
             scratch_shapes=scratch,
             compiler_params=pltpu.CompilerParams(
                 collective_id=0, has_side_effects=True, vmem_limit_bytes=48 * 2**20
             ),
         )(
+            *[
+                pltpu.with_memory_space_constraint(x, pltpu.HBM)
+                for x in (
             cycle_modes,
             global_now.reshape(192, LANES),
             global_prev.reshape(192, LANES),
@@ -839,7 +854,19 @@
             regional_prev.reshape(96, LANES),
             moduli.reshape(32, LANES),
             inv_mass.reshape(32, LANES),
-        )
+            )]
+        )
+        two, slab, force = pl.pallas_call(
+            copy_out,
+            out_shape=[
+                jax.ShapeDtypeStruct((192, LANES), F32),
+                jax.ShapeDtypeStruct((96, LANES), F32),
+                jax.ShapeDtypeStruct((96, LANES), F32),
+            ],
+            in_specs=[hbm] * 3,
+            out_specs=[hbm] * 3,
+            scratch_shapes=[pltpu.SemaphoreType.DMA((3,))],
+        )(two, slab, force)
         return (
             two.reshape(global_now.shape),
             slab.reshape(regional_now.shape),

time: 48.6 us -> 45.6 us (0.938)
  local copies, waits for them, and re-layouts: 10.4 us -> 1.87 us
  Pallas kernels: 36.9 us -> 42.9 us
    unnamed x33 -> x6, local copies, waits for them, and re-layouts: 10.4 us -> 1.87 us
    pallas_call x0 -> x1, Pallas kernels: none -> 7.08 us  [on_device(): pl.pallas_call(copy_out, out_shape=[jax.ShapeDtypeStruct((192, LANES), F3...]
    pallas_call x1, Pallas kernels: 36.9 us -> 35.8 us  [on_device(): pl.pallas_call(functools.partial(kernel, (n_gx, n_gy, n_gz)), out_shape=[...]
where the time goes in v1:
time: 45.6 us; the launch traced here: 45.4 us
  Pallas kernels  42.9 us (94%)
  local copies, waits for them, and re-layouts  1.87 us (4%)
  between operations  0.66 us (1%)
    pallas_call x1, Pallas kernels, on_device(): pl.pallas_call(functools.partial(kernel, (n_gx, n_gy, n_gz)), out_shape=[...  35.8 us
    pallas_call x1, Pallas kernels, on_device(): pl.pallas_call(copy_out, out_shape=[jax.ShapeDtypeStruct((192, LANES), F3...  7.08 us
    unnamed x6, local copies, waits for them, and re-layouts  1.87 us

profile of v1, /device:TPU:1, one launch (start us, length us, event | category | flops | bytes accessed | tf_op | source)
XLA Modules:
  0.0 45.4 jit_solution(14085039681504210704)
XLA Ops:
  0.6 35.8 %shard_map.166 = (f32[192,128]{1,0:T(8,128)S(1)}, f32[96,128]{1,0:T(8,128)S(1)}, f32[96,128]{1,0:T(8,128)S(1)}) custom-call(s32[8]{0:T(128)} %modes_in.1, f32[192,128]{1,0:T(8,128)} %bitcast.10, f32[192,128]{1,0:T(8,128)} %bitcast.11, f32[8,128]{1,0:T(8,128)} %speed_in.1, f32[8,128]{1,0:T(8,128)} %radius_in.1, f32[128,128]{1,0:T(8,128)} %second_in.1, ...), custom_call_target="tpu_custom_call" | custom-call | tf_op jit(solution)/shard_map/pallas_call | solution.py:825
  36.5 0.0 copy-start
  36.5 0.6 %copy-done = f32[192,128]{1,0:T(8,128)} copy-done((f32[192,128]{1,0:T(8,128)}, f32[192,128]{1,0:T(8,128)S(1)}, u32[]{:S(2)}) %copy-start) | copy-done | bytes 98328
  37.1 0.0 copy-start.1
  37.1 0.6 %copy-done.1 = f32[96,128]{1,0:T(8,128)} copy-done((f32[96,128]{1,0:T(8,128)}, f32[96,128]{1,0:T(8,128)S(1)}, u32[]{:S(2)}) %copy-start.1) | copy-done | bytes 49176
  37.7 0.0 copy-start.2
  37.7 0.6 %copy-done.2 = f32[96,128]{1,0:T(8,128)} copy-done((f32[96,128]{1,0:T(8,128)}, f32[96,128]{1,0:T(8,128)S(1)}, u32[]{:S(2)}) %copy-start.2) | copy-done | bytes 49176
  38.3 7.1 %shard_map.167 = (f32[192,128]{1,0:T(8,128)}, f32[96,128]{1,0:T(8,128)}, f32[96,128]{1,0:T(8,128)}) custom-call(f32[192,128]{1,0:T(8,128)} %copy-done, f32[96,128]{1,0:T(8,128)} %copy-done.1, f32[96,128]{1,0:T(8,128)} %copy-done.2), custom_call_target="tpu_custom_call" | custom-call | tf_op jit(solution)/shard_map/pallas_call | solution.py:859
Async XLA Ops:
  36.5 0.6 %copy-start = (f32[192,128]{1,0:T(8,128)}, f32[192,128]{1,0:T(8,128)S(1)}, u32[]{:S(2)}) copy-start(f32[192,128]{1,0:T(8,128)S(1)} %get-tuple-element.9.refs_0_) | copy-start | bytes 294916
  37.1 0.6 %copy-start.1 = (f32[96,128]{1,0:T(8,128)}, f32[96,128]{1,0:T(8,128)S(1)}, u32[]{:S(2)}) copy-start(f32[96,128]{1,0:T(8,128)S(1)} %get-tuple-element.10.refs_1_) | copy-start | bytes 147460
  37.7 0.6 %copy-start.2 = (f32[96,128]{1,0:T(8,128)}, f32[96,128]{1,0:T(8,128)S(1)}, u32[]{:S(2)}) copy-start(f32[96,128]{1,0:T(8,128)S(1)} %get-tuple-element.11.refs_2_) | copy-start | bytes 147460

commit v2 on v1

--- a/solution.py
+++ b/solution.py
@@ -743,15 +743,6 @@
     for copy in sent:
         copy.wait_send()
     for copy in outs:
-        copy.wait()
-
-
-def copy_out(*refs):
-    sems = refs[6]
-    copies = [pltpu.make_async_copy(refs[i], refs[3 + i], sems.at[i]) for i in range(3)]
-    for copy in copies:
-        copy.start()
-    for copy in copies:
         copy.wait()
 
 
@@ -856,17 +847,6 @@
             inv_mass.reshape(32, LANES),
             )]
         )
-        two, slab, force = pl.pallas_call(
-            copy_out,
-            out_shape=[
-                jax.ShapeDtypeStruct((192, LANES), F32),
-                jax.ShapeDtypeStruct((96, LANES), F32),
-                jax.ShapeDtypeStruct((96, LANES), F32),
-            ],
-            in_specs=[hbm] * 3,
-            out_specs=[hbm] * 3,
-            scratch_shapes=[pltpu.SemaphoreType.DMA((3,))],
-        )(two, slab, force)
         return (
             two.reshape(global_now.shape),
             slab.reshape(regional_now.shape),

time: 45.6 us -> 38.5 us (0.84)
  Pallas kernels: 42.9 us -> 35.8 us
    pallas_call x1 -> x0, Pallas kernels: 7.08 us -> none  [on_device(): pl.pallas_call(copy_out, out_shape=[jax.ShapeDtypeStruct((192, LANES), F3...]
    unnamed x6 -> x3, local copies, waits for them, and re-layouts: 1.87 us -> 1.88 us
where the time goes in v2:
time: 38.5 us; the launch traced here: 38.3 us
  Pallas kernels  35.8 us (93%)
  local copies, waits for them, and re-layouts  1.88 us (5%)
  between operations  0.65 us (2%)
    pallas_call x1, Pallas kernels, on_device(): pl.pallas_call(functools.partial(kernel, (n_gx, n_gy, n_gz)), out_shape=[...  35.8 us
    unnamed x3, local copies, waits for them, and re-layouts  1.88 us

profile of v2, /device:TPU:1, one launch (start us, length us, event | category | flops | bytes accessed | tf_op | source)
XLA Modules:
  0.0 38.3 jit_solution(14255743847521484936)
XLA Ops:
  0.6 35.8 %shard_map.166 = (f32[192,128]{1,0:T(8,128)S(1)}, f32[96,128]{1,0:T(8,128)S(1)}, f32[96,128]{1,0:T(8,128)S(1)}) custom-call(s32[8]{0:T(128)} %modes_in.1, f32[192,128]{1,0:T(8,128)} %bitcast.13, f32[192,128]{1,0:T(8,128)} %bitcast.14, f32[8,128]{1,0:T(8,128)} %speed_in.1, f32[8,128]{1,0:T(8,128)} %radius_in.1, f32[128,128]{1,0:T(8,128)} %second_in.1, ...), custom_call_target="tpu_custom_call" | custom-call | tf_op jit(solution)/shard_map/pallas_call | solution.py:816
  36.5 0.6 %copy.21 = f32[4,6,8,128]{3,2,1,0:T(8,128)} copy(f32[4,6,8,128]{3,2,1,0:T(8,128)S(1)} %bitcast.10) | data formatting | bytes 196608
  37.1 0.6 %copy.22 = f32[3,4,8,128]{3,2,1,0:T(8,128)} copy(f32[3,4,8,128]{3,2,1,0:T(8,128)S(1)} %bitcast.12) | data formatting | bytes 98304
  37.7 0.6 %copy.23 = f32[3,4,8,128]{3,2,1,0:T(8,128)} copy(f32[3,4,8,128]{3,2,1,0:T(8,128)S(1)} %bitcast.11) | data formatting | bytes 98304

commit v3 on v2

--- a/solution.py
+++ b/solution.py
@@ -161,6 +161,7 @@
     face_sems,
     group_sems,
     owner_sems,
+    ring_sems,
 ):
     n_gx, n_gy, n_gz = sizes
     gx, gy, gz = lax.axis_index("gx"), lax.axis_index("gy"), lax.axis_index("gz")
@@ -195,7 +196,7 @@
 
     barrier = pltpu.get_barrier_semaphore()
     for axis, steps in (
-        ("gx", range(1, n_gx)),
+        ("gx", sorted({1, n_gx - 1})),
         ("gy", range(1, n_gy)),
         ("gz", sorted({1, n_gz - 1})),
     ):
@@ -203,7 +204,7 @@
             pl.semaphore_signal(
                 barrier, inc=1, device_id=away(axis, step), device_id_type=MESH
             )
-    greeted = n_gx - 1 + n_gy - 1 + len({1, n_gz - 1})
+    greeted = len({1, n_gx - 1}) + n_gy - 1 + len({1, n_gz - 1})
 
     def push(src, dst, sems, index, device):
         copy = pltpu.make_async_remote_copy(
@@ -246,6 +247,18 @@
 
     pl.semaphore_wait(barrier, greeted)
 
+    reaches = [reach for reach in (1, 2, 4) if 2 * reach < n_gx]
+
+    def tell(level):
+        for step in (reaches[level], -reaches[level]):
+            pl.semaphore_signal(
+                ring_sems.at[level], inc=1, device_id=away("gx", step), device_id_type=MESH
+            )
+
+    def hear(level):
+        pl.semaphore_wait(ring_sems.at[level], 2)
+
+    tell(0)
     sent = []
     cycle_in = []
     for side, step in ((0, -1), (1, 1)):
@@ -303,6 +316,10 @@
         [jnp.sum(tail * mu[x], axis=1, keepdims=True) for x in range(4)]
     )
     moduli_copies = send_faces(0, 1, 8)
+
+    hear(0)
+    if len(reaches) > 1:
+        tell(1)
 
     loads["second"].wait()
     pair_second[...] = operator_pair(second_ref[...])
@@ -458,6 +475,11 @@
             )
         )
     group_in = sent[-(n_gy - 1) :]
+
+    if len(reaches) > 1:
+        hear(1)
+    if len(reaches) > 2:
+        tell(2)
 
     for copy in moduli_copies:
         copy.wait_recv()
@@ -667,6 +689,8 @@
         )
         outgoing = jnp.where(lanes16 >> 3 == c, moved, outgoing)
     owner_send[...] = outgoing.reshape(n_gx, 1, LANES)
+    if len(reaches) > 2:
+        hear(2)
     for step in range(1, n_gx):
         peer = away("gx", step)
         sent.append(
@@ -811,6 +835,7 @@
             pltpu.SemaphoreType.DMA((2, 3, 6)),
             pltpu.SemaphoreType.DMA((2, n_gy)),
             pltpu.SemaphoreType.DMA((2, n_gx)),
+            pltpu.SemaphoreType.REGULAR((3,)),
         ]
         hbm = pl.BlockSpec(memory_space=pl.ANY)
         two, slab, force = pl.pallas_call(

time: 38.5 us -> 35.4 us (0.919)
  Pallas kernels: 35.8 us -> 32.8 us
    pallas_call x1, Pallas kernels: 35.8 us -> 32.8 us  [on_device(): pl.pallas_call(functools.partial(kernel, (n_gx, n_gy, n_gz)), out_shape=[...]
where the time goes in v3:
time: 35.4 us; the launch traced here: 35.3 us
  Pallas kernels  32.8 us (93%)
  local copies, waits for them, and re-layouts  1.88 us (5%)
  between operations  0.65 us (2%)
    pallas_call x1, Pallas kernels, on_device(): pl.pallas_call(functools.partial(kernel, (n_gx, n_gy, n_gz)), out_shape=[...  32.8 us
    unnamed x3, local copies, waits for them, and re-layouts  1.88 us

profile of v3, /device:TPU:1, one launch (start us, length us, event | category | flops | bytes accessed | tf_op | source)
XLA Modules:
  0.0 35.3 jit_solution(14504009425708857984)
XLA Ops:
  0.6 32.8 %shard_map.166 = (f32[192,128]{1,0:T(8,128)S(1)}, f32[96,128]{1,0:T(8,128)S(1)}, f32[96,128]{1,0:T(8,128)S(1)}) custom-call(s32[8]{0:T(128)} %modes_in.1, f32[192,128]{1,0:T(8,128)} %bitcast.13, f32[192,128]{1,0:T(8,128)} %bitcast.14, f32[8,128]{1,0:T(8,128)} %speed_in.1, f32[8,128]{1,0:T(8,128)} %radius_in.1, f32[128,128]{1,0:T(8,128)} %second_in.1, ...), custom_call_target="tpu_custom_call" | custom-call | tf_op jit(solution)/shard_map/pallas_call | solution.py:841
  33.4 0.6 %copy.21 = f32[4,6,8,128]{3,2,1,0:T(8,128)} copy(f32[4,6,8,128]{3,2,1,0:T(8,128)S(1)} %bitcast.10) | data formatting | bytes 196608
  34.0 0.6 %copy.22 = f32[3,4,8,128]{3,2,1,0:T(8,128)} copy(f32[3,4,8,128]{3,2,1,0:T(8,128)S(1)} %bitcast.12) | data formatting | bytes 98304
  34.7 0.6 %copy.23 = f32[3,4,8,128]{3,2,1,0:T(8,128)} copy(f32[3,4,8,128]{3,2,1,0:T(8,128)S(1)} %bitcast.11) | data formatting | bytes 98304

commit v4 on v3

--- a/solution.py
+++ b/solution.py
@@ -124,7 +124,6 @@
     moduli_ref,
     mass_ref,
     one_ref,
-    two_ref,
     edge_ref,
     pair_second,
     pair_first,
@@ -133,9 +132,7 @@
     slot_ref,
     mark_ref,
     base_ref,
-    force_ref,
     step_ref,
-    last_ref,
     band_z,
     band_y,
     band_x,
@@ -156,7 +153,6 @@
     owner_send,
     owner_recv,
     in_sem,
-    out_sem,
     cycle_sems,
     face_sems,
     group_sems,
@@ -195,16 +191,27 @@
         return {axis: lax.rem(index + step + count, count)}
 
     barrier = pltpu.get_barrier_semaphore()
-    for axis, steps in (
-        ("gx", sorted({1, n_gx - 1})),
-        ("gy", range(1, n_gy)),
-        ("gz", sorted({1, n_gz - 1})),
-    ):
-        for step in steps:
+    for step in range(1, n_gy):
+        pl.semaphore_signal(barrier, inc=1, device_id=away("gy", step), device_id_type=MESH)
+    there = {
+        ("gx", -1): gx > 0,
+        ("gx", 1): gx < n_gx - 1,
+        ("gy", -1): gy > 0,
+        ("gy", 1): gy < n_gy - 1,
+        ("gz", -1): gz > 0,
+        ("gz", 1): gz < n_gz - 1,
+    }
+    greeted = n_gy - 1 + len({1, n_gx - 1})
+    for step in sorted({1, n_gx - 1}):
+        pl.semaphore_signal(barrier, inc=1, device_id=away("gx", step), device_id_type=MESH)
+    for step in (-1, 1):
+        greeted = greeted + there["gz", step].astype(jnp.int32)
+
+        @pl.when(there["gz", step])
+        def _(step=step):
             pl.semaphore_signal(
-                barrier, inc=1, device_id=away(axis, step), device_id_type=MESH
+                barrier, inc=1, device_id=away("gz", step), device_id_type=MESH
             )
-    greeted = len({1, n_gx - 1}) + n_gy - 1 + len({1, n_gz - 1})
 
     def push(src, dst, sems, index, device):
         copy = pltpu.make_async_remote_copy(
@@ -217,6 +224,37 @@
         )
         copy.start()
         return copy
+
+    class Neighbour:
+        def __init__(self, src, dst, sems, index, axis, step):
+            self.copy = pltpu.make_async_remote_copy(
+                src_ref=src,
+                dst_ref=dst,
+                send_sem=sems.at[(0, *index)],
+                recv_sem=sems.at[(1, *index)],
+                device_id=away(axis, step),
+                device_id_type=MESH,
+            )
+            self.sends, self.receives = there[axis, step], there[axis, -step]
+            pl.when(self.sends)(lambda: self.copy.start())
+
+        def wait_recv(self):
+            pl.when(self.receives)(lambda: self.copy.wait_recv())
+
+        def wait_send(self):
+            pl.when(self.sends)(lambda: self.copy.wait_send())
+
+    for (axis, step), here in there.items():
+
+        @pl.when(jnp.logical_not(here))
+        def _(axis=axis, side=(1 - step) // 2):
+            if axis == "gx":
+                cycle_recv[side] = jnp.zeros(cycle_recv.shape[1:], F32)
+                x_recv[:, side] = jnp.zeros((3, 3, 8, LANES), F32)
+            elif axis == "gy":
+                y_recv[:, side] = jnp.zeros((3, 16, LANES), F32)
+            else:
+                z_recv[:, side] = jnp.zeros((3, 8, LANES), F32)
 
     sub = iota((8, LANES), 0)
     lane = iota((8, LANES), 1)
@@ -262,8 +300,8 @@
     sent = []
     cycle_in = []
     for side, step in ((0, -1), (1, 1)):
-        copy = push(
-            cycle_send.at[side], cycle_recv.at[side], cycle_sems, (side,), away("gx", step)
+        copy = Neighbour(
+            cycle_send.at[side], cycle_recv.at[side], cycle_sems, (side,), "gx", step
         )
         sent.append(copy)
         cycle_in.append(copy)
@@ -286,7 +324,7 @@
                 )
             ):
                 copies.append(
-                    push(src, dst, face_sems, (number, 2 * place + side), away(axis, step))
+                    Neighbour(src, dst, face_sems, (number, 2 * place + side), axis, step)
                 )
         sent.extend(copies)
         return copies
@@ -429,9 +467,7 @@
         edge_ref[pl.ds(edge, 24, stride=8), :] = beyond[side]
     two = section_sum(one, now_ref[...]) + side_weight * edge_ref[...].reshape(4, 6, 8, LANES)
     two = two.reshape(192, LANES)
-    two_ref[...] = two
-    outs = [pltpu.make_async_copy(two_ref, g_out, out_sem.at[0])]
-    outs[0].start()
+    g_out[...] = two
 
     coef = coupling * times_operator(two, pair_first) + (coupling * impedance / time_step) * (
         two - one
@@ -741,9 +777,7 @@
     force = dot_rows(
         jnp.concatenate([high, low], axis=1), jnp.concatenate([on_lane, on_lane], axis=1)
     )
-    force_ref[...] = force
-    outs.append(pltpu.make_async_copy(force_ref, force_out, out_sem.at[1]))
-    outs[1].start()
+    force_out[...] = force
     for x in range(4):
         scale = slab_factor * mass_ref[8 * x : 8 * x + 8, :]
         for c in range(3):
@@ -757,16 +791,21 @@
         scale = slab_factor * mass_ref[8 * x : 8 * x + 8, :]
         for c in range(3):
             at = 32 * c + 8 * x
-            last_ref[at : at + 8, :] = (
+            slab_out[at : at + 8, :] = (
                 2.0 * step_ref[at : at + 8, :]
                 - slab_ref[at : at + 8, :]
-                + scale * (force_ref[at : at + 8, :] - around[x][c])
+                + scale * (force_out[at : at + 8, :] - around[x][c])
             )
-    outs.append(pltpu.make_async_copy(last_ref, slab_out, out_sem.at[2]))
-    outs[2].start()
     for copy in sent:
         copy.wait_send()
-    for copy in outs:
+
+
+def copy_out(*refs):
+    sems = refs[6]
+    copies = [pltpu.make_async_copy(refs[i], refs[3 + i], sems.at[i]) for i in range(3)]
+    for copy in copies:
+        copy.start()
+    for copy in copies:
         copy.wait()
 
 
@@ -799,15 +838,12 @@
         scratch += [
             pltpu.VMEM((192, LANES), F32),
             pltpu.VMEM((192, LANES), F32),
-            pltpu.VMEM((192, LANES), F32),
             pltpu.VMEM((2 * LANES, 2 * LANES), BF16),
             pltpu.VMEM((2 * LANES, 2 * LANES), BF16),
             pltpu.VMEM((2 * LANES, points), BF16),
             pltpu.VMEM((8, 8, points), F32),
             pltpu.VMEM((LANES, points), BF16),
             pltpu.VMEM((8, LANES), F32),
-            pltpu.VMEM((96, LANES), F32),
-            pltpu.VMEM((96, LANES), F32),
             pltpu.VMEM((96, LANES), F32),
             pltpu.VMEM((96, LANES), F32),
             pltpu.VMEM((9, 4, 8, LANES), F32),
@@ -830,7 +866,6 @@
             pltpu.VMEM((n_gx, 1, LANES), F32),
             pltpu.VMEM((n_gx, 1, LANES), F32),
             pltpu.SemaphoreType.DMA((15,)),
-            pltpu.SemaphoreType.DMA((3,)),
             pltpu.SemaphoreType.DMA((2, 2)),
             pltpu.SemaphoreType.DMA((2, 3, 6)),
             pltpu.SemaphoreType.DMA((2, n_gy)),
@@ -846,7 +881,7 @@
                 pltpu.VMEM((96, LANES), F32),
             ],
             in_specs=[hbm] * 15,
-            out_specs=[hbm] * 3,
+            out_specs=[pl.BlockSpec(memory_space=pltpu.VMEM)] * 3,
             scratch_shapes=scratch,
             compiler_params=pltpu.CompilerParams(
                 collective_id=0, has_side_effects=True, vmem_limit_bytes=48 * 2**20
@@ -872,6 +907,17 @@
             inv_mass.reshape(32, LANES),
             )]
         )
+        two, slab, force = pl.pallas_call(
+            copy_out,
+            out_shape=[
+                pltpu.HBM((192, LANES), F32),
+                pltpu.HBM((96, LANES), F32),
+                pltpu.HBM((96, LANES), F32),
+            ],
+            in_specs=[hbm] * 3,
+            out_specs=[hbm] * 3,
+            scratch_shapes=[pltpu.SemaphoreType.DMA((3,))],
+        )(*[pltpu.with_memory_space_constraint(x, pltpu.VMEM) for x in (two, slab, force)])
         return (
             two.reshape(global_now.shape),
             slab.reshape(regional_now.shape),

time: 35.4 us -> 33.2 us (0.938)
  local copies, waits for them, and re-layouts: 1.88 us -> 0 us
  Pallas kernels: 32.8 us -> 32.4 us
    unnamed x3 -> x0, local copies, waits for them, and re-layouts: 1.88 us -> none
    pallas_call x1, Pallas kernels: 32.8 us -> 31.7 us  [on_device(): pl.pallas_call(functools.partial(kernel, (n_gx, n_gy, n_gz)), out_shape=[...]
    pallas_call x0 -> x1, Pallas kernels: none -> 0.7 us  [on_device(): pl.pallas_call(copy_out, out_shape=[pltpu.HBM((192, LANES), F32), pltpu.H...]
where the time goes in v4:
time: 33.2 us; the launch traced here: 33 us
  Pallas kernels  32.4 us (98%)
  between operations  0.64 us (2%)
    pallas_call x1, Pallas kernels, on_device(): pl.pallas_call(functools.partial(kernel, (n_gx, n_gy, n_gz)), out_shape=[...  31.7 us
    pallas_call x1, Pallas kernels, on_device(): pl.pallas_call(copy_out, out_shape=[pltpu.HBM((192, LANES), F32), pltpu.H...  0.7 us

profile of v4, /device:TPU:1, one launch (start us, length us, event | category | flops | bytes accessed | tf_op | source)
XLA Modules:
  0.0 33.0 jit_solution(8259492374476791815)
XLA Ops:
  0.6 31.7 %shard_map.166 = (f32[192,128]{1,0:T(8,128)S(1)}, f32[96,128]{1,0:T(8,128)S(1)}, f32[96,128]{1,0:T(8,128)S(1)}) custom-call(s32[8]{0:T(128)} %modes_in.1, f32[192,128]{1,0:T(8,128)} %bitcast.10, f32[192,128]{1,0:T(8,128)} %bitcast.11, f32[8,128]{1,0:T(8,128)} %speed_in.1, f32[8,128]{1,0:T(8,128)} %radius_in.1, f32[128,128]{1,0:T(8,128)} %second_in.1, ...), custom_call_target="tpu_custom_call" | custom-call | tf_op jit(solution)/shard_map/pallas_call | solution.py:876
  32.3 0.7 %shard_map.167 = (f32[192,128]{1,0:T(8,128)}, f32[96,128]{1,0:T(8,128)}, f32[96,128]{1,0:T(8,128)}) custom-call(f32[192,128]{1,0:T(8,128)S(1)} %get-tuple-element.9.refs_0_, f32[96,128]{1,0:T(8,128)S(1)} %get-tuple-element.10.refs_1_, f32[96,128]{1,0:T(8,128)S(1)} %get-tuple-element.11.refs_2_), custom_call_target="tpu_custom_call" | custom-call | tf_op jit(solution)/shard_map/pallas_call | solution.py:910

commit v5 on v4

--- a/solution.py
+++ b/solution.py
@@ -162,6 +162,8 @@
     n_gx, n_gy, n_gz = sizes
     gx, gy, gz = lax.axis_index("gx"), lax.axis_index("gy"), lax.axis_index("gz")
     points = dest_ref.shape[1]
+    core, chip = lax.rem(gy, 2), lax.div(gy, 2)
+    chips = n_gy // 2
 
     loads = {}
     for number, (name, src, dst) in enumerate(
@@ -285,7 +287,10 @@
 
     pl.semaphore_wait(barrier, greeted)
 
-    reaches = [reach for reach in (1, 2, 4) if 2 * reach < n_gx]
+    reaches, known = [], 0
+    while known < n_gx // 2:
+        reaches.append(min(known + 1, n_gx // 2 - known))
+        known += reaches[-1]
 
     def tell(level):
         for step in (reaches[level], -reaches[level]):
@@ -295,6 +300,12 @@
 
     def hear(level):
         pl.semaphore_wait(ring_sems.at[level], 2)
+
+    def advance(level):
+        if level < len(reaches):
+            hear(level)
+        if level + 1 < len(reaches):
+            tell(level + 1)
 
     tell(0)
     sent = []
@@ -355,9 +366,19 @@
     )
     moduli_copies = send_faces(0, 1, 8)
 
-    hear(0)
-    if len(reaches) > 1:
-        tell(1)
+    chain = min(n_gx - 1, 10)
+
+    @pl.when((gx > 0) & (gx <= chain))
+    def _():
+        pl.semaphore_wait(ring_sems.at[len(reaches)], 1)
+
+    @pl.when(gx < chain)
+    def _():
+        pl.semaphore_signal(
+            ring_sems.at[len(reaches)], inc=1, device_id=away("gx", 1), device_id_type=MESH
+        )
+
+    advance(0)
 
     loads["second"].wait()
     pair_second[...] = operator_pair(second_ref[...])
@@ -416,15 +437,11 @@
     slot = owner_x * RANKS + rank
     slot_ref[...] = (iota((LANES, points), 0) == slot).astype(F32).astype(BF16)
     target = target_ref[...]
-    mine = jnp.where(owner_y == gy, F32(1.0), F32(0.0))
     sub_p = iota((8, points), 0)
-    marks = jnp.where(
-        sub_p == 0,
-        (target >> 7).astype(F32) * mine,
-        jnp.where(sub_p == 1, (target & 127).astype(F32) * mine, F32(0.0)),
-    )
-    marked = dot_rows(marks.astype(BF16), slot_ref[...])
-    mark_ref[...] = jnp.broadcast_to(128.0 * marked[0:1] + marked[1:2], (8, LANES))
+    mine = owner_y == 2 * (sub_p & 3) + core
+    marks = jnp.where(sub_p < 4, target >> 7, target & 127).astype(F32)
+    marked = dot_rows(jnp.where(mine, marks, F32(0.0)).astype(BF16), slot_ref[...])
+    mark_ref[0:4, :] = (128.0 / chips) * marked[0:4] + (1.0 / chips) * marked[4:8]
     source = source_ref[...]
     picked = (iota((LANES, points), 0) == (source & 127)).astype(F32).astype(BF16)
     pick_ref[0:LANES, :] = picked
@@ -444,6 +461,8 @@
     loads["first"].wait()
     pair_first[...] = operator_pair(first_ref[...])
 
+    advance(1)
+
     for copy in cycle_in:
         copy.wait_recv()
     flags = (last_x, has_x)
@@ -487,35 +506,79 @@
             jnp.broadcast_to(jnp.sum(total, axis=0, keepdims=True), (8, points)),
             values,
         )
+    half = 8 * max(1, chips // 2)
     by_group = jnp.concatenate(
         [
-            jnp.where(owner_y == 2 * t + (sub_p >> 2), values, F32(0.0))
-            for t in range(n_gy // 2)
+            jnp.where(owner_y == 2 * (2 * tile + (sub_p >> 2)) + side, values, F32(0.0))
+            for side in range(2)
+            for tile in range(half // 8)
         ],
         axis=0,
     )
     high, low = halves(by_group)
     packed = dot_rows(jnp.concatenate([high, low], axis=0), slot_ref[...])
-    packed = packed[: 4 * n_gy] + packed[4 * n_gy :]
-    for group in range(n_gy):
-        group_send[group] = packed[4 * group : 4 * group + 4]
-    for step in range(1, n_gy):
-        peer = away("gy", step)
-        sent.append(
-            push(
-                group_send.at[peer["gy"]],
-                group_recv.at[step],
-                group_sems,
-                (step,),
-                peer,
+    packed = packed[: 2 * half] + packed[2 * half :]
+    for side in range(2):
+        group_send[side] = packed[half * side : half * side + half]
+    pair = push(
+        group_send.at[1 - core], group_recv, group_sems, (), {"gy": gy + 1 - 2 * core}
+    )
+    sent.append(pair)
+
+    pair.wait_recv()
+    total = group_send[core] + group_recv[...]
+    rows16 = iota((n_gx, LANES), 0)
+    lanes16 = iota((n_gx, LANES), 1)
+    for place in range(chips):
+        outgoing = jnp.zeros((n_gx, LANES), F32)
+        for c in range(4):
+            at = 4 * place + c
+            line = total[at : at + 1] if c < 3 else mark_ref[place : place + 1]
+            line = jnp.broadcast_to(line, (8, LANES))
+            if (RANKS * (c + 1 - n_gx)) % LANES:
+                line = pltpu.roll(line, (RANKS * (c + 1 - n_gx)) % LANES, 1)
+            moved = pltpu.roll(
+                jnp.broadcast_to(line[0:1], (n_gx, LANES)), 0, 1, stride=RANKS, stride_axis=0
             )
-        )
-    group_in = sent[-(n_gy - 1) :]
-
-    if len(reaches) > 1:
-        hear(1)
-    if len(reaches) > 2:
-        tell(2)
+            outgoing = jnp.where(lanes16 >> 3 == c, moved, outgoing)
+        owner_send[place] = outgoing.reshape(n_gx, 1, LANES)
+
+    def to_row(a):
+        for b in range(chips):
+            if a or b:
+                peer_x, peer_chip = away("gx", a)["gx"], lax.rem(chip + b, chips)
+                pltpu.make_async_remote_copy(
+                    src_ref=owner_send.at[peer_chip, n_gx - 1 - peer_x],
+                    dst_ref=owner_recv.at[b * n_gx + a],
+                    send_sem=owner_sems.at[0],
+                    recv_sem=owner_sems.at[1],
+                    device_id={"gx": peer_x, "gy": 2 * peer_chip + core},
+                    device_id_type=MESH,
+                ).start()
+
+    far_first = sorted(range(n_gx), key=lambda a: -min(a, n_gx - a))
+    early = {a: (gx <= chain) & (gx + a >= n_gx) for a in far_first}
+    for a in far_first:
+        pl.when(early[a])(functools.partial(to_row, a))
+    first = min(2, len(reaches) - 1)
+    for level in range(first, len(reaches)):
+        if level >= 2:
+            advance(level)
+        reach = sum(reaches[: level + 1])
+        for a in far_first:
+            distance = min(a, n_gx - a)
+            if distance <= reach and (level == first or distance > reach - reaches[level]):
+                pl.when(jnp.logical_not(early[a]))(functools.partial(to_row, a))
+    owner_recv[0] = owner_send[chip, n_gx - 1 - gx]
+    rows_all = chips * n_gx
+    owner_in = pltpu.make_async_remote_copy(
+        src_ref=owner_recv.at[1:rows_all],
+        dst_ref=owner_recv.at[1:rows_all],
+        send_sem=owner_sems.at[0],
+        recv_sem=owner_sems.at[1],
+        device_id=away("gx", 1),
+        device_id_type=MESH,
+    )
 
     for copy in moduli_copies:
         copy.wait_recv()
@@ -707,40 +770,6 @@
     loads["slab"].wait()
     now_copies = face_values(1, slab_ref)
 
-    for copy in group_in:
-        copy.wait_recv()
-    total = group_send[gy]
-    for step in range(1, n_gy):
-        total = total + group_recv[step]
-    rows16 = iota((n_gx, LANES), 0)
-    lanes16 = iota((n_gx, LANES), 1)
-    outgoing = jnp.zeros((n_gx, LANES), F32)
-    for c in range(4):
-        line = total[c : c + 1] if c < 3 else mark_ref[0:1]
-        line = jnp.broadcast_to(line, (8, LANES))
-        if (RANKS * (c + 1 - n_gx)) % LANES:
-            line = pltpu.roll(line, (RANKS * (c + 1 - n_gx)) % LANES, 1)
-        moved = pltpu.roll(
-            jnp.broadcast_to(line[0:1], (n_gx, LANES)), 0, 1, stride=RANKS, stride_axis=0
-        )
-        outgoing = jnp.where(lanes16 >> 3 == c, moved, outgoing)
-    owner_send[...] = outgoing.reshape(n_gx, 1, LANES)
-    if len(reaches) > 2:
-        hear(2)
-    for step in range(1, n_gx):
-        peer = away("gx", step)
-        sent.append(
-            push(
-                owner_send.at[n_gx - 1 - peer["gx"]],
-                owner_recv.at[step],
-                owner_sems,
-                (step,),
-                peer,
-            )
-        )
-    owner_in = sent[-(n_gx - 1) :]
-    owner_recv[0] = owner_send[n_gx - 1 - gx]
-
     inside = inner_stiffness(slab_ref)
     loads["before"].wait()
     loads["mass"].wait()
@@ -755,9 +784,10 @@
                 - scale * around[x][c]
             )
 
-    for copy in owner_in:
-        copy.wait_recv()
-    arrived = owner_recv[...].reshape(n_gx, LANES)
+    owner_in.wait_recv()
+    arrived = sum(
+        owner_recv[b * n_gx : (b + 1) * n_gx].reshape(n_gx, LANES) for b in range(chips)
+    )
     lines = []
     moved = pltpu.roll(arrived, 0, 1, stride=RANKS, stride_axis=0)
     for c in range(4):
@@ -798,6 +828,7 @@
             )
     for copy in sent:
         copy.wait_send()
+    owner_in.wait_send()
 
 
 def copy_out(*refs):
@@ -861,16 +892,16 @@
             pltpu.VMEM((3, 2, 16, LANES), F32),
             pltpu.VMEM((3, 2, 8, LANES), F32),
             pltpu.VMEM((3, 2, 8, LANES), F32),
-            pltpu.VMEM((n_gy, 4, LANES), F32),
-            pltpu.VMEM((n_gy, 4, LANES), F32),
-            pltpu.VMEM((n_gx, 1, LANES), F32),
-            pltpu.VMEM((n_gx, 1, LANES), F32),
+            pltpu.VMEM((2, 8 * max(1, n_gy // 4), LANES), F32),
+            pltpu.VMEM((8 * max(1, n_gy // 4), LANES), F32),
+            pltpu.VMEM((n_gy // 2, n_gx, 1, LANES), F32),
+            pltpu.VMEM((n_gy // 2 * n_gx, 1, LANES), F32),
             pltpu.SemaphoreType.DMA((15,)),
             pltpu.SemaphoreType.DMA((2, 2)),
             pltpu.SemaphoreType.DMA((2, 3, 6)),
-            pltpu.SemaphoreType.DMA((2, n_gy)),
-            pltpu.SemaphoreType.DMA((2, n_gx)),
-            pltpu.SemaphoreType.REGULAR((3,)),
+            pltpu.SemaphoreType.DMA((2,)),
+            pltpu.SemaphoreType.DMA((2,)),
+            pltpu.SemaphoreType.REGULAR((5,)),
         ]
         hbm = pl.BlockSpec(memory_space=pl.ANY)
         two, slab, force = pl.pallas_call(

time: 33.2 us -> 40.7 us (1.23)
  the two profiles are of different devices: /device:TPU:1 before, /device:TPU:80 now
where the time goes in v5:
time: 40.7 us; the launch traced here: 40.6 us
  Pallas kernels  39.9 us (98%)
  between operations  0.64 us (2%)
    pallas_call x1, Pallas kernels, on_device(): pl.pallas_call(functools.partial(kernel, (n_gx, n_gy, n_gz)), out_shape=[...  39.2 us

profile of v5, /device:TPU:80, one launch (start us, length us, event | category | flops | bytes accessed | tf_op | source)
XLA Modules:
  0.0 40.6 jit_solution(6739433955587422097)
XLA Ops:
  0.6 39.2 %shard_map.166 = (f32[192,128]{1,0:T(8,128)S(1)}, f32[96,128]{1,0:T(8,128)S(1)}, f32[96,128]{1,0:T(8,128)S(1)}) custom-call(s32[8]{0:T(128)} %modes_in.1, f32[192,128]{1,0:T(8,128)} %bitcast.10, f32[192,128]{1,0:T(8,128)} %bitcast.11, f32[8,128]{1,0:T(8,128)} %speed_in.1, f32[8,128]{1,0:T(8,128)} %radius_in.1, f32[128,128]{1,0:T(8,128)} %second_in.1, ...), custom_call_target="tpu_custom_call" | custom-call | tf_op jit(solution)/shard_map/pallas_call | solution.py:907
  39.9 0.7 %shard_map.167 = (f32[192,128]{1,0:T(8,128)}, f32[96,128]{1,0:T(8,128)}, f32[96,128]{1,0:T(8,128)}) custom-call(f32[192,128]{1,0:T(8,128)S(1)} %get-tuple-element.9.refs_0_, f32[96,128]{1,0:T(8,128)S(1)} %get-tuple-element.10.refs_1_, f32[96,128]{1,0:T(8,128)S(1)} %get-tuple-element.11.refs_2_), custom_call_target="tpu_custom_call" | custom-call | tf_op jit(solution)/shard_map/pallas_call | solution.py:941

commit v6 on v5

--- a/solution.py
+++ b/solution.py
@@ -165,6 +165,42 @@
     core, chip = lax.rem(gy, 2), lax.div(gy, 2)
     chips = n_gy // 2
 
+    def away(axis, step):
+        index, count = {"gx": (gx, n_gx), "gy": (gy, n_gy), "gz": (gz, n_gz)}[axis]
+        return {axis: lax.rem(index + step + count, count)}
+
+    barrier = pltpu.get_barrier_semaphore()
+    for step in range(1, n_gy):
+        pl.semaphore_signal(barrier, inc=1, device_id=away("gy", step), device_id_type=MESH)
+    there = {
+        ("gx", -1): gx > 0,
+        ("gx", 1): gx < n_gx - 1,
+        ("gy", -1): gy > 0,
+        ("gy", 1): gy < n_gy - 1,
+        ("gz", -1): gz > 0,
+        ("gz", 1): gz < n_gz - 1,
+    }
+    greeted = n_gy - 1 + chips * len({1, n_gx - 1})
+    for step in sorted({1, n_gx - 1}):
+        for b in range(chips):
+            pl.semaphore_signal(
+                barrier,
+                inc=1,
+                device_id={
+                    "gx": away("gx", step)["gx"],
+                    "gy": 2 * lax.rem(chip + b, chips) + core,
+                },
+                device_id_type=MESH,
+            )
+    for step in (-1, 1):
+        greeted = greeted + there["gz", step].astype(jnp.int32)
+
+        @pl.when(there["gz", step])
+        def _(step=step):
+            pl.semaphore_signal(
+                barrier, inc=1, device_id=away("gz", step), device_id_type=MESH
+            )
+
     loads = {}
     for number, (name, src, dst) in enumerate(
         (
@@ -188,33 +224,6 @@
         loads[name] = pltpu.make_async_copy(src, dst, in_sem.at[number])
         loads[name].start()
 
-    def away(axis, step):
-        index, count = {"gx": (gx, n_gx), "gy": (gy, n_gy), "gz": (gz, n_gz)}[axis]
-        return {axis: lax.rem(index + step + count, count)}
-
-    barrier = pltpu.get_barrier_semaphore()
-    for step in range(1, n_gy):
-        pl.semaphore_signal(barrier, inc=1, device_id=away("gy", step), device_id_type=MESH)
-    there = {
-        ("gx", -1): gx > 0,
-        ("gx", 1): gx < n_gx - 1,
-        ("gy", -1): gy > 0,
-        ("gy", 1): gy < n_gy - 1,
-        ("gz", -1): gz > 0,
-        ("gz", 1): gz < n_gz - 1,
-    }
-    greeted = n_gy - 1 + len({1, n_gx - 1})
-    for step in sorted({1, n_gx - 1}):
-        pl.semaphore_signal(barrier, inc=1, device_id=away("gx", step), device_id_type=MESH)
-    for step in (-1, 1):
-        greeted = greeted + there["gz", step].astype(jnp.int32)
-
-        @pl.when(there["gz", step])
-        def _(step=step):
-            pl.semaphore_signal(
-                barrier, inc=1, device_id=away("gz", step), device_id_type=MESH
-            )
-
     def push(src, dst, sems, index, device):
         copy = pltpu.make_async_remote_copy(
             src_ref=src,
@@ -287,9 +296,9 @@
 
     pl.semaphore_wait(barrier, greeted)
 
-    reaches, known = [], 0
+    reaches, known = [], 1
     while known < n_gx // 2:
-        reaches.append(min(known + 1, n_gx // 2 - known))
+        reaches.append(min(known, n_gx // 2 - known))
         known += reaches[-1]
 
     def tell(level):
@@ -324,19 +333,20 @@
     has_y = jnp.where(gy > 0, F32(1.0), F32(0.0))
     has_z = jnp.where(gz > 0, F32(1.0), F32(0.0))
 
-    def send_faces(number, x_count, y_count):
-        copies = []
-        for side, step in ((0, -1), (1, 1)):
-            for place, (axis, src, dst) in enumerate(
-                (
-                    ("gx", x_send.at[number, side, 0:x_count], x_recv.at[number, side, 0:x_count]),
-                    ("gy", y_send.at[number, side, 0:y_count], y_recv.at[number, side, 0:y_count]),
-                    ("gz", z_send.at[number, side], z_recv.at[number, side]),
-                )
-            ):
-                copies.append(
-                    Neighbour(src, dst, face_sems, (number, 2 * place + side), axis, step)
-                )
+    def send_face(number, axis, count):
+        place = ("gx", "gy", "gz").index(axis)
+        out, into = ((x_send, x_recv), (y_send, y_recv), (z_send, z_recv))[place]
+        copies = [
+            Neighbour(
+                out.at[number, side, 0:count],
+                into.at[number, side, 0:count],
+                face_sems,
+                (number, 2 * place + side),
+                axis,
+                step,
+            )
+            for side, step in ((0, -1), (1, 1))
+        ]
         sent.extend(copies)
         return copies
 
@@ -364,19 +374,11 @@
     z_send[0, 1] = columns_to_lanes(
         [jnp.sum(tail * mu[x], axis=1, keepdims=True) for x in range(4)]
     )
-    moduli_copies = send_faces(0, 1, 8)
-
-    chain = min(n_gx - 1, 10)
-
-    @pl.when((gx > 0) & (gx <= chain))
-    def _():
-        pl.semaphore_wait(ring_sems.at[len(reaches)], 1)
-
-    @pl.when(gx < chain)
-    def _():
-        pl.semaphore_signal(
-            ring_sems.at[len(reaches)], inc=1, device_id=away("gx", 1), device_id_type=MESH
-        )
+    moduli_copies = [
+        copy
+        for axis, count in (("gy", 8), ("gz", 8), ("gx", 1))
+        for copy in send_face(0, axis, count)
+    ]
 
     advance(0)
 
@@ -543,32 +545,37 @@
             outgoing = jnp.where(lanes16 >> 3 == c, moved, outgoing)
         owner_send[place] = outgoing.reshape(n_gx, 1, LANES)
 
-    def to_row(a):
-        for b in range(chips):
-            if a or b:
-                peer_x, peer_chip = away("gx", a)["gx"], lax.rem(chip + b, chips)
-                pltpu.make_async_remote_copy(
-                    src_ref=owner_send.at[peer_chip, n_gx - 1 - peer_x],
-                    dst_ref=owner_recv.at[b * n_gx + a],
-                    send_sem=owner_sems.at[0],
-                    recv_sem=owner_sems.at[1],
-                    device_id={"gx": peer_x, "gy": 2 * peer_chip + core},
-                    device_id_type=MESH,
-                ).start()
-
-    far_first = sorted(range(n_gx), key=lambda a: -min(a, n_gx - a))
-    early = {a: (gx <= chain) & (gx + a >= n_gx) for a in far_first}
-    for a in far_first:
-        pl.when(early[a])(functools.partial(to_row, a))
-    first = min(2, len(reaches) - 1)
-    for level in range(first, len(reaches)):
-        if level >= 2:
-            advance(level)
-        reach = sum(reaches[: level + 1])
-        for a in far_first:
-            distance = min(a, n_gx - a)
-            if distance <= reach and (level == first or distance > reach - reaches[level]):
-                pl.when(jnp.logical_not(early[a]))(functools.partial(to_row, a))
+    def to_row(a, first=0):
+        peer_x = lax.rem(gx + a, n_gx)
+        for b in range(first, chips):
+            peer_chip = lax.rem(chip + b, chips)
+            pltpu.make_async_remote_copy(
+                src_ref=owner_send.at[peer_chip, n_gx - 1 - peer_x],
+                dst_ref=owner_recv.at[b * n_gx + a],
+                send_sem=owner_sems.at[0],
+                recv_sem=owner_sems.at[1],
+                device_id={"gx": peer_x, "gy": 2 * peer_chip + core},
+                device_id_type=MESH,
+            ).start()
+
+    def far_first(first, last, when=None):
+        def body(number, carry):
+            away_by = (number + 1) // 2
+            a = n_gx // 2 + jnp.where(number % 2 == 1, -away_by, away_by)
+            if when is None:
+                to_row(a)
+            else:
+                pl.when(when(a))(lambda: to_row(a))
+            return carry
+
+        lax.fori_loop(first, last, body, 0)
+
+    near = n_gx // 2 - 1 if n_gx > 8 else 0
+    far_first(near, n_gx - 1)
+    to_row(0, 1)
+    for level in range(2, len(reaches)):
+        advance(level)
+    far_first(0, near)
     owner_recv[0] = owner_send[chip, n_gx - 1 - gx]
     rows_all = chips * n_gx
     owner_in = pltpu.make_async_remote_copy(
@@ -699,14 +706,16 @@
 
     def face_values(number, ref):
         field = ref[...].reshape(3, 4, 8, LANES)
-        for c in range(3):
-            x_send[number, 0, c] = field[c, 0]
-            x_send[number, 1, c] = sum(coupling_x(i, 4) * field[c, i] for i in range(4))
         y_send[number, 0, 0:12] = ref[pl.ds(0, 12, stride=8), :]
         part_ref[...] = (over_y[...][None] * field).reshape(96, LANES)
         y_send[number, 1, 0:12] = sum(
             part_ref[pl.ds(4 + k, 12, stride=8), :] for k in range(4)
         )
+        copies = send_face(number, "gy", 16)
+        for c in range(3):
+            x_send[number, 0, c] = field[c, 0]
+            x_send[number, 1, c] = sum(coupling_x(i, 4) * field[c, i] for i in range(4))
+        copies += send_face(number, "gx", 3)
         z_send[number, 0] = columns_to_lanes(
             [field[c, x][:, 0:1] for c in range(3) for x in range(4)]
         )
@@ -717,7 +726,7 @@
                 for x in range(4)
             ]
         )
-        return send_faces(number, 3, 16)
+        return copies + send_face(number, "gz", 8)
 
     def inner_stiffness(ref):
         field = ref[...].reshape(3, 4, 8, LANES)

time: 40.7 us -> 32.9 us (0.81)
  the two profiles are of different devices: /device:TPU:80 before, /device:TPU:1 now
where the time goes in v6:
time: 32.9 us; the launch traced here: 32.8 us
  Pallas kernels  32.1 us (98%)
  between operations  0.64 us (2%)
    pallas_call x1, Pallas kernels, on_device(): pl.pallas_call(functools.partial(kernel, (n_gx, n_gy, n_gz)), out_shape=[...  31.4 us
    pallas_call x1, Pallas kernels, on_device(): pl.pallas_call(copy_out, out_shape=[pltpu.HBM((192, LANES), F32), pltpu.H...  0.7 us

profile of v6, /device:TPU:1, one launch (start us, length us, event | category | flops | bytes accessed | tf_op | source)
XLA Modules:
  0.0 32.8 jit_solution(2793540560200207405)
XLA Ops:
  0.6 31.4 %shard_map.166 = (f32[192,128]{1,0:T(8,128)S(1)}, f32[96,128]{1,0:T(8,128)S(1)}, f32[96,128]{1,0:T(8,128)S(1)}) custom-call(s32[8]{0:T(128)} %modes_in.1, f32[192,128]{1,0:T(8,128)} %bitcast.10, f32[192,128]{1,0:T(8,128)} %bitcast.11, f32[8,128]{1,0:T(8,128)} %speed_in.1, f32[8,128]{1,0:T(8,128)} %radius_in.1, f32[128,128]{1,0:T(8,128)} %second_in.1, ...), custom_call_target="tpu_custom_call" | custom-call | tf_op jit(solution)/shard_map/pallas_call | solution.py:916
  32.1 0.7 %shard_map.167 = (f32[192,128]{1,0:T(8,128)}, f32[96,128]{1,0:T(8,128)}, f32[96,128]{1,0:T(8,128)}) custom-call(f32[192,128]{1,0:T(8,128)S(1)} %get-tuple-element.9.refs_0_, f32[96,128]{1,0:T(8,128)S(1)} %get-tuple-element.10.refs_1_, f32[96,128]{1,0:T(8,128)S(1)} %get-tuple-element.11.refs_2_), custom_call_target="tpu_custom_call" | custom-call | tf_op jit(solution)/shard_map/pallas_call | solution.py:950

commit v7 on v6

--- a/solution.py
+++ b/solution.py
@@ -180,18 +180,20 @@
         ("gz", -1): gz > 0,
         ("gz", 1): gz < n_gz - 1,
     }
-    greeted = n_gy - 1 + chips * len({1, n_gx - 1})
+    greeted = n_gy - 1 + len({1, n_gx - 1}) + jnp.where(gx == 1, chips - 1, 0)
     for step in sorted({1, n_gx - 1}):
-        for b in range(chips):
+        pl.semaphore_signal(barrier, inc=1, device_id=away("gx", step), device_id_type=MESH)
+
+    @pl.when(gx == 0)
+    def _():
+        for b in range(1, chips):
             pl.semaphore_signal(
                 barrier,
                 inc=1,
-                device_id={
-                    "gx": away("gx", step)["gx"],
-                    "gy": 2 * lax.rem(chip + b, chips) + core,
-                },
+                device_id={"gx": 1, "gy": 2 * lax.rem(chip + b, chips) + core},
                 device_id_type=MESH,
             )
+
     for step in (-1, 1):
         greeted = greeted + there["gz", step].astype(jnp.int32)
 
@@ -296,9 +298,9 @@
 
     pl.semaphore_wait(barrier, greeted)
 
-    reaches, known = [], 1
+    reaches, known = [], 0
     while known < n_gx // 2:
-        reaches.append(min(known, n_gx // 2 - known))
+        reaches.append(min(known + 1, n_gx // 2 - known))
         known += reaches[-1]
 
     def tell(level):
@@ -316,7 +318,21 @@
         if level + 1 < len(reaches):
             tell(level + 1)
 
+    told_last = min(9, n_gx - 1)
+
+    def hear_below():
+        pl.semaphore_wait(ring_sems.at[4], 1)
+
+    def pass_on(first, last):
+        @pl.when((gx >= first) & (gx <= min(last, told_last - 1)))
+        def _():
+            pl.when(gx >= 2)(hear_below)
+            pl.semaphore_signal(
+                ring_sems.at[4], inc=1, device_id=away("gx", 1), device_id_type=MESH
+            )
+
     tell(0)
+    pass_on(1, 4)
     sent = []
     cycle_in = []
     for side, step in ((0, -1), (1, 1)):
@@ -380,6 +396,7 @@
         for copy in send_face(0, axis, count)
     ]
 
+    pass_on(5, 7)
     advance(0)
 
     loads["second"].wait()
@@ -464,6 +481,7 @@
     pair_first[...] = operator_pair(first_ref[...])
 
     advance(1)
+    pass_on(8, 8)
 
     for copy in cycle_in:
         copy.wait_recv()
@@ -570,12 +588,26 @@
 
         lax.fori_loop(first, last, body, 0)
 
-    near = n_gx // 2 - 1 if n_gx > 8 else 0
-    far_first(near, n_gx - 1)
-    to_row(0, 1)
-    for level in range(2, len(reaches)):
-        advance(level)
-    far_first(0, near)
+    pl.when(gx == told_last)(hear_below)
+    chained = (gx >= min(8, told_last)) & (gx <= told_last)
+
+    def below(a):
+        return chained & (gx + a >= n_gx)
+
+    def others(a):
+        return jnp.logical_not(below(a))
+
+    pl.when(chained)(lambda: far_first(0, n_gx - 1, below))
+    first = min(1, len(reaches) - 1)
+    done = n_gx - 1
+    for level in range(first, len(reaches)):
+        if level >= 2:
+            advance(level)
+        start = max(0, 2 * (n_gx // 2 - sum(reaches[: level + 1])) - 1)
+        far_first(start, done, others)
+        done = start
+        if level == first:
+            to_row(0, 1)
     owner_recv[0] = owner_send[chip, n_gx - 1 - gx]
     rows_all = chips * n_gx
     owner_in = pltpu.make_async_remote_copy(

time: 32.9 us -> 33 us (level)
  the two profiles are of different devices: /device:TPU:1 before, /device:TPU:32 now
where the time goes in v7:
time: 33 us; the launch traced here: 32.9 us
  Pallas kernels  32.2 us (98%)
  between operations  0.64 us (2%)
    pallas_call x1, Pallas kernels, on_device(): pl.pallas_call(functools.partial(kernel, (n_gx, n_gy, n_gz)), out_shape=[...  31.5 us
    pallas_call x1, Pallas kernels, on_device(): pl.pallas_call(copy_out, out_shape=[pltpu.HBM((192, LANES), F32), pltpu.H...  0.7 us

profile of v7, /device:TPU:32, one launch (start us, length us, event | category | flops | bytes accessed | tf_op | source)
XLA Modules:
  0.0 32.9 jit_solution(9240579131253754353)
XLA Ops:
  0.6 31.5 %shard_map.166 = (f32[192,128]{1,0:T(8,128)S(1)}, f32[96,128]{1,0:T(8,128)S(1)}, f32[96,128]{1,0:T(8,128)S(1)}) custom-call(s32[8]{0:T(128)} %modes_in.1, f32[192,128]{1,0:T(8,128)} %bitcast.10, f32[192,128]{1,0:T(8,128)} %bitcast.11, f32[8,128]{1,0:T(8,128)} %speed_in.1, f32[8,128]{1,0:T(8,128)} %radius_in.1, f32[128,128]{1,0:T(8,128)} %second_in.1, ...), custom_call_target="tpu_custom_call" | custom-call | tf_op jit(solution)/shard_map/pallas_call | solution.py:948
  32.2 0.7 %shard_map.167 = (f32[192,128]{1,0:T(8,128)}, f32[96,128]{1,0:T(8,128)}, f32[96,128]{1,0:T(8,128)}) custom-call(f32[192,128]{1,0:T(8,128)S(1)} %get-tuple-element.9.refs_0_, f32[96,128]{1,0:T(8,128)S(1)} %get-tuple-element.10.refs_1_, f32[96,128]{1,0:T(8,128)S(1)} %get-tuple-element.11.refs_2_), custom_call_target="tpu_custom_call" | custom-call | tf_op jit(solution)/shard_map/pallas_call | solution.py:982

commit v8 on v6

--- a/solution.py
+++ b/solution.py
@@ -316,7 +316,21 @@
         if level + 1 < len(reaches):
             tell(level + 1)
 
+    told_last = min(9, n_gx - 1)
+
+    def hear_below():
+        pl.semaphore_wait(ring_sems.at[4], 1)
+
+    def pass_on(first, last):
+        @pl.when((gx >= first) & (gx <= min(last, told_last - 1)))
+        def _():
+            pl.when(gx >= 2)(hear_below)
+            pl.semaphore_signal(
+                ring_sems.at[4], inc=1, device_id=away("gx", 1), device_id_type=MESH
+            )
+
     tell(0)
+    pass_on(1, 4)
     sent = []
     cycle_in = []
     for side, step in ((0, -1), (1, 1)):
@@ -380,6 +394,7 @@
         for copy in send_face(0, axis, count)
     ]
 
+    pass_on(5, 7)
     advance(0)
 
     loads["second"].wait()
@@ -464,6 +479,7 @@
     pair_first[...] = operator_pair(first_ref[...])
 
     advance(1)
+    pass_on(8, 8)
 
     for copy in cycle_in:
         copy.wait_recv()
@@ -570,23 +586,19 @@
 
         lax.fori_loop(first, last, body, 0)
 
+    pl.when(gx == told_last)(hear_below)
+    chained = (gx >= min(8, told_last)) & (gx <= told_last)
+
+    def below(a):
+        return chained & (gx + a >= n_gx)
+
+    def others(a):
+        return jnp.logical_not(below(a))
+
     near = n_gx // 2 - 1 if n_gx > 8 else 0
+    pl.when(chained)(lambda: far_first(0, near, below))
     far_first(near, n_gx - 1)
     to_row(0, 1)
-    for level in range(2, len(reaches)):
-        advance(level)
-    far_first(0, near)
-    owner_recv[0] = owner_send[chip, n_gx - 1 - gx]
-    rows_all = chips * n_gx
-    owner_in = pltpu.make_async_remote_copy(
-        src_ref=owner_recv.at[1:rows_all],
-        dst_ref=owner_recv.at[1:rows_all],
-        send_sem=owner_sems.at[0],
-        recv_sem=owner_sems.at[1],
-        device_id=away("gx", 1),
-        device_id_type=MESH,
-    )
-
     for copy in moduli_copies:
         copy.wait_recv()
     mu_next_x = last_x * x_recv[0, 0, 0]
@@ -778,6 +790,20 @@
     spread_ref[...] = jnp.zeros((96, LANES), F32)
     loads["slab"].wait()
     now_copies = face_values(1, slab_ref)
+
+    for level in range(2, len(reaches)):
+        advance(level)
+    far_first(0, near, others)
+    owner_recv[0] = owner_send[chip, n_gx - 1 - gx]
+    rows_all = chips * n_gx
+    owner_in = pltpu.make_async_remote_copy(
+        src_ref=owner_recv.at[1:rows_all],
+        dst_ref=owner_recv.at[1:rows_all],
+        send_sem=owner_sems.at[0],
+        recv_sem=owner_sems.at[1],
+        device_id=away("gx", 1),
+        device_id_type=MESH,
+    )
 
     inside = inner_stiffness(slab_ref)
     loads["before"].wait()

time: 32.9 us -> 32.5 us (0.988)
  Pallas kernels: 32.1 us -> 31.7 us
    pallas_call x1, Pallas kernels: 31.4 us -> 31 us  [on_device(): pl.pallas_call(functools.partial(kernel, (n_gx, n_gy, n_gz)), out_shape=[...]
where the time goes in v8:
time: 32.5 us; the launch traced here: 32.4 us
  Pallas kernels  31.7 us (98%)
  between operations  0.64 us (2%)
    pallas_call x1, Pallas kernels, on_device(): pl.pallas_call(functools.partial(kernel, (n_gx, n_gy, n_gz)), out_shape=[...  31 us
    pallas_call x1, Pallas kernels, on_device(): pl.pallas_call(copy_out, out_shape=[pltpu.HBM((192, LANES), F32), pltpu.H...  0.7 us

profile of v8, /device:TPU:1, one launch (start us, length us, event | category | flops | bytes accessed | tf_op | source)
XLA Modules:
  0.0 32.4 jit_solution(14715821622804116889)
XLA Ops:
  0.6 31.0 %shard_map.166 = (f32[192,128]{1,0:T(8,128)S(1)}, f32[96,128]{1,0:T(8,128)S(1)}, f32[96,128]{1,0:T(8,128)S(1)}) custom-call(s32[8]{0:T(128)} %modes_in.1, f32[192,128]{1,0:T(8,128)} %bitcast.10, f32[192,128]{1,0:T(8,128)} %bitcast.11, f32[8,128]{1,0:T(8,128)} %speed_in.1, f32[8,128]{1,0:T(8,128)} %radius_in.1, f32[128,128]{1,0:T(8,128)} %second_in.1, ...), custom_call_target="tpu_custom_call" | custom-call | tf_op jit(solution)/shard_map/pallas_call | solution.py:942
  31.7 0.7 %shard_map.167 = (f32[192,128]{1,0:T(8,128)}, f32[96,128]{1,0:T(8,128)}, f32[96,128]{1,0:T(8,128)}) custom-call(f32[192,128]{1,0:T(8,128)S(1)} %get-tuple-element.9.refs_0_, f32[96,128]{1,0:T(8,128)S(1)} %get-tuple-element.10.refs_1_, f32[96,128]{1,0:T(8,128)S(1)} %get-tuple-element.11.refs_2_), custom_call_target="tpu_custom_call" | custom-call | tf_op jit(solution)/shard_map/pallas_call | solution.py:976

commit v9 on v8

--- a/solution.py
+++ b/solution.py
@@ -316,7 +316,7 @@
         if level + 1 < len(reaches):
             tell(level + 1)
 
-    told_last = min(9, n_gx - 1)
+    told_last = min(10, n_gx - 1)
 
     def hear_below():
         pl.semaphore_wait(ring_sems.at[4], 1)
@@ -586,6 +586,7 @@
 
         lax.fori_loop(first, last, body, 0)
 
+    pass_on(9, 9)
     pl.when(gx == told_last)(hear_below)
     chained = (gx >= min(8, told_last)) & (gx <= told_last)
 

time: 32.5 us -> 32.1 us (0.988)
  Pallas kernels: 31.7 us -> 31.3 us
    pallas_call x1, Pallas kernels: 31 us -> 30.6 us  [on_device(): pl.pallas_call(functools.partial(kernel, (n_gx, n_gy, n_gz)), out_shape=[...]
where the time goes in v9:
time: 32.1 us; the launch traced here: 32 us
  Pallas kernels  31.3 us (98%)
  between operations  0.64 us (2%)
    pallas_call x1, Pallas kernels, on_device(): pl.pallas_call(functools.partial(kernel, (n_gx, n_gy, n_gz)), out_shape=[...  30.6 us
    pallas_call x1, Pallas kernels, on_device(): pl.pallas_call(copy_out, out_shape=[pltpu.HBM((192, LANES), F32), pltpu.H...  0.7 us

profile of v9, /device:TPU:1, one launch (start us, length us, event | category | flops | bytes accessed | tf_op | source)
XLA Modules:
  0.0 32.0 jit_solution(10575331324563466320)
XLA Ops:
  0.6 30.6 %shard_map.166 = (f32[192,128]{1,0:T(8,128)S(1)}, f32[96,128]{1,0:T(8,128)S(1)}, f32[96,128]{1,0:T(8,128)S(1)}) custom-call(s32[8]{0:T(128)} %modes_in.1, f32[192,128]{1,0:T(8,128)} %bitcast.10, f32[192,128]{1,0:T(8,128)} %bitcast.11, f32[8,128]{1,0:T(8,128)} %speed_in.1, f32[8,128]{1,0:T(8,128)} %radius_in.1, f32[128,128]{1,0:T(8,128)} %second_in.1, ...), custom_call_target="tpu_custom_call" | custom-call | tf_op jit(solution)/shard_map/pallas_call | solution.py:943
  31.3 0.7 %shard_map.167 = (f32[192,128]{1,0:T(8,128)}, f32[96,128]{1,0:T(8,128)}, f32[96,128]{1,0:T(8,128)}) custom-call(f32[192,128]{1,0:T(8,128)S(1)} %get-tuple-element.9.refs_0_, f32[96,128]{1,0:T(8,128)S(1)} %get-tuple-element.10.refs_1_, f32[96,128]{1,0:T(8,128)S(1)} %get-tuple-element.11.refs_2_), custom_call_target="tpu_custom_call" | custom-call | tf_op jit(solution)/shard_map/pallas_call | solution.py:977

commit v10 on v9

--- a/solution.py
+++ b/solution.py
@@ -596,7 +596,7 @@
     def others(a):
         return jnp.logical_not(below(a))
 
-    near = n_gx // 2 - 1 if n_gx > 8 else 0
+    near = n_gx // 2 + 3 if n_gx > 8 else 0
     pl.when(chained)(lambda: far_first(0, near, below))
     far_first(near, n_gx - 1)
     to_row(0, 1)

time: 32.1 us -> 32.1 us (level)
  no operation moved by 1% of the time
where the time goes in v10:
time: 32.1 us; the launch traced here: 32 us
  Pallas kernels  31.3 us (98%)
  between operations  0.64 us (2%)
    pallas_call x1, Pallas kernels, on_device(): pl.pallas_call(functools.partial(kernel, (n_gx, n_gy, n_gz)), out_shape=[...  30.6 us
    pallas_call x1, Pallas kernels, on_device(): pl.pallas_call(copy_out, out_shape=[pltpu.HBM((192, LANES), F32), pltpu.H...  0.7 us

profile of v10, /device:TPU:1, one launch (start us, length us, event | category | flops | bytes accessed | tf_op | source)
XLA Modules:
  0.0 32.0 jit_solution(3008277056153021003)
XLA Ops:
  0.6 30.6 %shard_map.166 = (f32[192,128]{1,0:T(8,128)S(1)}, f32[96,128]{1,0:T(8,128)S(1)}, f32[96,128]{1,0:T(8,128)S(1)}) custom-call(s32[8]{0:T(128)} %modes_in.1, f32[192,128]{1,0:T(8,128)} %bitcast.10, f32[192,128]{1,0:T(8,128)} %bitcast.11, f32[8,128]{1,0:T(8,128)} %speed_in.1, f32[8,128]{1,0:T(8,128)} %radius_in.1, f32[128,128]{1,0:T(8,128)} %second_in.1, ...), custom_call_target="tpu_custom_call" | custom-call | tf_op jit(solution)/shard_map/pallas_call | solution.py:943
  31.3 0.7 %shard_map.167 = (f32[192,128]{1,0:T(8,128)}, f32[96,128]{1,0:T(8,128)}, f32[96,128]{1,0:T(8,128)}) custom-call(f32[192,128]{1,0:T(8,128)S(1)} %get-tuple-element.9.refs_0_, f32[96,128]{1,0:T(8,128)S(1)} %get-tuple-element.10.refs_1_, f32[96,128]{1,0:T(8,128)S(1)} %get-tuple-element.11.refs_2_), custom_call_target="tpu_custom_call" | custom-call | tf_op jit(solution)/shard_map/pallas_call | solution.py:977
